TPU v7x, 512 devices: a whole 4x4x16 slice. The times are simulated.
512 devices in a mesh: head: 2 (over y_hi), inner: 32 (over y_lo, z), outer: 8 (over x, core).
Axes of the slice: x: 4, y: 4 (y_hi: 2, y_lo: 2; y = y_hi * 2 + y_lo), z: 16, core: 2. Of those that a mesh axis runs over, the one named last changes fastest.
Arguments:
- queries: bfloat16 [32768, 4096], P(('head', 'inner', 'outer')), may hold values from -6 to 6
- keys: bfloat16 [32768, 512], P(('head', 'inner', 'outer')), may hold values from -6 to 6
- values: bfloat16 [32768, 512], P(('head', 'inner', 'outer')), may hold values from -6 to 6
- block_order: int32 [2, 32, 8], replicated, may hold values from 0 to 511, as said below
Outputs:
- attended: bfloat16 [32768, 4096], P(('head', 'inner', 'outer'))
Inputs may be any that keep to these rules, and one draw needn't show every extreme that they name: A permutation of the blocks: for each i and o, block_order[0, i, o] = o * 2 * 32 + c and block_order[1, i, o] = o * 2 * 32 + 2 * 32 - 1 - c, where c runs over a permutation of 0 to 31 for each o.
All inputs are finite; a program needn't handle non-finite values.
Results may differ from a plain program's by a relative error of at most 0.008.
Values may be sent and summed in bfloat16 or wider, within the bound.
No kernel may reach another device: no remote copies, remote signals or barrier semaphores. Data moves between devices by JAX's collectives and lax.ppermute only.
A program may use at most 64 MiB of HBM per device.

v0:
```python
import math

import jax
import jax.numpy as jnp
from jax import lax
from jax.sharding import PartitionSpec as P

HD = 128


very_low = -1e30


def shifted(block, axis, distance):
    devices = range(lax.axis_size(axis))
    route = [(i - distance, i) for i in devices if i - distance in devices]
    return lax.ppermute(block, axis, route)


def fold_block(running, query_heads, key_block, value_block, visible):
    run_max, run_total, run_sum = running
    key_count = key_block.shape[0]
    kv_count = query_heads.shape[1]
    key_heads = key_block.reshape(key_count, kv_count, HD)
    value_heads = value_block.reshape(key_count, kv_count, HD)
    scores = jnp.einsum(
        "rkgd,nkd->kgrn", query_heads, key_heads, preferred_element_type=jnp.float32
    ) * (1.0 / math.sqrt(HD))
    scores = jnp.where(visible[None, None], scores, very_low)
    new_max = jnp.maximum(run_max, jnp.max(scores, axis=-1))
    weights = jnp.where(visible[None, None], jnp.exp(scores - new_max[..., None]), 0.0)
    factor = jnp.exp(run_max - new_max)
    new_total = run_total * factor + jnp.sum(weights, axis=-1)
    new_sum = run_sum * factor[..., None] + jnp.einsum(
        "kgrn,nkd->kgrd",
        weights.astype(jnp.bfloat16),
        value_heads,
        preferred_element_type=jnp.float32,
    )
    return (new_max, new_total, new_sum)


def fold_keys(
    running, query_heads, query_position, key_block, value_block, key_position, key_allowed
):
    count = key_block.shape[0]
    width_block = math.gcd(count, 512)
    steps = count // width_block
    columns = key_block.shape[1]

    def one_block(carry, pieces):
        block_key, block_value, block_position, block_allowed = pieces
        visible = (block_position[None, :] <= query_position[:, None]) & block_allowed[None, :]
        return (fold_block(carry, query_heads, block_key, block_value, visible), None)

    running, unused = lax.scan(
        one_block,
        running,
        (
            key_block.reshape(steps, width_block, columns),
            value_block.reshape(steps, width_block, columns),
            key_position.reshape(steps, width_block),
            key_allowed.reshape(steps, width_block),
        ),
    )
    return running


def body(queries, keys, values, block_order):
    tok_count = queries.shape[0]
    inner_count = lax.axis_size("inner")
    outer_count = lax.axis_size("outer")
    local_query, local_key, local_value = (
        lax.all_to_all(queries, "head", split_axis=1, concat_axis=0, tiled=True),
        lax.all_to_all(keys, "head", split_axis=1, concat_axis=0, tiled=True),
        lax.all_to_all(values, "head", split_axis=1, concat_axis=0, tiled=True),
    )
    row_count = local_query.shape[0]
    columns = local_key.shape[1]
    kv_count = columns // HD
    group_size = local_query.shape[1] // HD // kv_count
    query_heads = local_query.reshape(row_count, kv_count, group_size, HD)
    outer_now = lax.axis_index("outer")
    inner_now = lax.axis_index("inner")
    outer_pick = (jnp.arange(outer_count, dtype=jnp.int32) == outer_now).astype(jnp.int32)
    order_table = jnp.sum(block_order * outer_pick[None, None, :], axis=2)
    flat_order = order_table.T.reshape(-1)
    inner_pick = (jnp.arange(inner_count, dtype=jnp.int32) == inner_now).astype(jnp.int32)
    own_blocks = jnp.sum(order_table * inner_pick[None, :], axis=1)
    query_position = (
        own_blocks[:, None] * tok_count + jnp.arange(tok_count, dtype=jnp.int32)[None, :]
    ).reshape(-1)
    block_ids = jnp.arange(flat_order.shape[0], dtype=jnp.int32)
    has_earlier = outer_now > 0
    running = (
        jnp.full((kv_count, group_size, row_count), very_low, jnp.float32),
        jnp.zeros((kv_count, group_size, row_count), jnp.float32),
        jnp.zeros((kv_count, group_size, row_count, HD), jnp.float32),
    )
    earlier_key, earlier_value = shifted(
        (local_key[tok_count:], local_value[tok_count:]), "outer", 1
    )
    key_block = lax.all_gather(local_key, "inner", axis=0, tiled=True)
    value_block = lax.all_gather(local_value, "inner", axis=0, tiled=True)
    key_index = jnp.arange(key_block.shape[0], dtype=jnp.int32)
    key_position = (
        jnp.sum(
            jnp.where(
                (key_index // tok_count)[:, None] == block_ids[None, :], flat_order[None, :], 0
            ),
            axis=1,
        )
        * tok_count
        + key_index % tok_count
    )
    key_allowed = jnp.ones((key_block.shape[0],), bool)
    running = fold_keys(
        running, query_heads, query_position, key_block, value_block, key_position, key_allowed
    )
    key_block = lax.all_gather(earlier_key, "inner", axis=0, tiled=True)
    value_block = lax.all_gather(earlier_value, "inner", axis=0, tiled=True)
    key_position = jnp.zeros((key_block.shape[0],), jnp.int32)
    key_allowed = jnp.broadcast_to(has_earlier, (key_block.shape[0],))
    running = fold_keys(
        running, query_heads, query_position, key_block, value_block, key_position, key_allowed
    )
    run_max, run_total, run_sum = running
    attended = (
        (run_sum / run_total[..., None])
        .transpose(2, 0, 1, 3)
        .reshape(row_count, -1)
        .astype(jnp.bfloat16)
    )
    return lax.all_to_all(attended, "head", split_axis=0, concat_axis=1, tiled=True)


def solution(mesh):
    in_specs = (
        P(("head", "inner", "outer"), None),
        P(("head", "inner", "outer"), None),
        P(("head", "inner", "outer"), None),
        P(),
    )
    out_specs = P(("head", "inner", "outer"), None)
    return jax.shard_map(body, mesh=mesh, in_specs=in_specs, out_specs=out_specs, check_vma=False)
```

profile of v0, /device:TPU:2, one launch (start us, length us, event | category | flops | bytes accessed | tf_op | source)
XLA Modules:
  0.0 594.0 jit_solution(17527984743989387902)
XLA Ops:
  7.4 10.0 %all_to_all.70 = bf16[64,2,256]{2,0,1:T(8,128)(2,1)} all-to-all(bf16[64,2,256]{2,0,1:T(8,128)(2,1)S(1)} %bitcast.142), channel_id=1, replica_groups=mesh['head'=2,'inner'=32,'outer'=8] {'head'}, dimensions={1} | all-to-all | bytes 131072 | tf_op jit(solution)/shard_map/all_to_all | solution.py:75
  18.3 8.6 %all_to_all.71 = bf16[64,2,256]{2,0,1:T(8,128)(2,1)} all-to-all(bf16[64,2,256]{2,0,1:T(8,128)(2,1)S(1)} %bitcast.143), channel_id=1, replica_groups=mesh['head'=2,'inner'=32,'outer'=8] {'head'}, dimensions={1} | all-to-all | bytes 131072 | tf_op jit(solution)/shard_map/all_to_all | solution.py:76
  27.8 1.9 collective-permute-start.1
  29.7 3.3 collective-permute-done.1
  33.6 1.9 copy.113
  35.5 3.5 all-to-all-start.1
  41.2 1.9 collective-permute-start
  43.2 3.3 collective-permute-done
  47.1 3.0 all-to-all-done.1
  50.3 103.4 %all-gather.5.cloned.1.call-done = bf16[4096,256]{1,0:T(8,128)(2,1)} async-done(((bf16[128,256]{1,0:T(8,128)(2,1)}), bf16[4096,256]{1,0:T(8,128)(2,1)}) %all-gather.5.cloned.1.call-update) | async-done | bytes 2097168 | tf_op jit(solution)/shard_map/all_gather | solution.py:103
  153.7 128.4 %all-gather.7.cloned.1.call-done = bf16[4096,256]{1,0:T(8,128)(2,1)} async-done(((bf16[128,256]{1,0:T(8,128)(2,1)}), bf16[4096,256]{1,0:T(8,128)(2,1)}) %all-gather.7.cloned.1.call-update) | async-done | bytes 2097168 | tf_op jit(solution)/shard_map/all_gather | solution.py:104
  282.1 92.5 %while.31 = (s32[]{:T(128)}, f32[2,8,128]{2,1,0:T(8,128)S(1)}, f32[2,8,128]{2,1,0:T(8,128)S(1)}, f32[2,8,128,128]{3,2,1,0:T(8,128)S(1)}, s32[8,512]{1,0:T(8,128)...) while((s32[]{:T(128)}, f32[2,8,128]{2,1,0:T(8,128)S(1)}, ...), condition=%wide.region_6.7_spmd.clone, body=%wide.region_3.6_spmd.clone.sunk | while | flops 551364736 | bytes 18227336 | solution.py:56
  282.4 1.1 constant_dynamic-slice_fusion.10
  283.6 2.8 fusion.67
  286.4 3.2 fusion.68
  289.7 3.9 fusion.70
  293.9 1.1 constant_dynamic-slice_fusion.10
  295.2 2.8 fusion.67
  297.9 3.2 fusion.68
  301.3 3.9 fusion.70
  305.5 1.1 constant_dynamic-slice_fusion.10
  306.7 2.8 fusion.67
  309.5 3.2 fusion.68
  312.8 3.9 fusion.70
  317.0 1.1 constant_dynamic-slice_fusion.10
  318.3 2.8 fusion.67
  321.0 3.2 fusion.68
  324.4 3.9 fusion.70
  328.6 1.1 constant_dynamic-slice_fusion.10
  329.8 2.8 fusion.67
  332.6 3.2 fusion.68
  336.0 3.9 fusion.70
  340.2 1.1 constant_dynamic-slice_fusion.10
  341.4 2.8 fusion.67
  344.2 3.2 fusion.68
  347.5 3.9 fusion.70
  351.7 1.1 constant_dynamic-slice_fusion.10
  353.0 2.8 fusion.67
  355.7 3.2 fusion.68
  359.1 3.9 fusion.70
  363.3 1.1 constant_dynamic-slice_fusion.10
  364.5 2.8 fusion.67
  367.3 3.2 fusion.68
  370.6 3.9 fusion.70
  374.5 34.9 %all-gather.11.cloned.1.call-done = bf16[2048,256]{1,0:T(8,128)(2,1)} async-done(((bf16[64,256]{1,0:T(8,128)(2,1)}), bf16[2048,256]{1,0:T(8,128)(2,1)}) %all-gather.11.cloned.1.call-update) | async-done | bytes 1048592 | tf_op jit(solution)/shard_map/all_gather | solution.py:121
  409.4 126.6 %all-gather.9.cloned.1.call-done = bf16[2048,256]{1,0:T(8,128)(2,1)} async-done(((bf16[64,256]{1,0:T(8,128)(2,1)}), bf16[2048,256]{1,0:T(8,128)(2,1)}) %all-gather.9.cloned.1.call-update) | async-done | bytes 1048592 | tf_op jit(solution)/shard_map/all_gather | solution.py:120
  536.0 37.8 %while.30 = (s32[]{:T(128)}, f32[2,8,128]{2,1,0:T(8,128)S(1)}, f32[2,8,128]{2,1,0:T(8,128)S(1)}, f32[2,8,128,128]{3,2,1,0:T(8,128)S(1)}, pred[4,512]{1,0:T(4,128...) while((s32[]{:T(128)}, f32[2,8,128]{2,1,0:T(8,128)S(1)}, ...), condition=%wide.region_10.11_spmd.clone, body=%wide.region_7.10_spmd.clone.sunk | while | flops 551096576 | bytes 34998416 | solution.py:56
  536.4 1.1 constant_dynamic-slice_fusion.8
  538.5 1.9 copy-done
  540.4 1.0 fusion.61
  541.6 3.9 fusion.62
  545.8 1.1 constant_dynamic-slice_fusion.8
  547.9 1.9 copy-done
  549.8 1.0 fusion.61
  551.0 3.9 fusion.62
  555.2 1.1 constant_dynamic-slice_fusion.8
  557.3 1.9 copy-done
  559.3 1.0 fusion.61
  560.5 3.9 fusion.62
  564.7 1.1 constant_dynamic-slice_fusion.8
  566.8 1.9 copy-done
  568.7 1.0 fusion.61
  569.9 3.9 fusion.62
  574.7 11.9 %all_to_all.72 = bf16[2,64,2048]{2,1,0:T(8,128)(2,1)S(1)} all-to-all(bf16[2,64,2048]{2,1,0:T(8,128)(2,1)S(1)} %convert_element_type.34), channel_id=1, replica_groups=mesh['head'=2,'inner'=32,'outer'=8] {'head'}, dimensions={0} | all-to-all | bytes 1048576 | tf_op jit(solution)/shard_map/all_to_all | solution.py:134
  (154 shorter events, 18.6 us)
Async XLA Ops:
  6.5 147.2 %all-gather.5.cloned.1.call-start = ((), (), s32[]{:S(2)}) async-start(), calls=%async_computation.4 | async-start | bytes 2162688 | tf_op jit(solution)/shard_map/all_gather | solution.py:103
  17.4 264.7 %all-gather.7.cloned.1.call-start = ((), (), s32[]{:S(2)}) async-start(), calls=%async_computation.5 | async-start | bytes 2162688 | tf_op jit(solution)/shard_map/all_gather | solution.py:104
  26.9 382.5 %all-gather.11.cloned.1.call-start = ((), (), s32[]{:S(2)}) async-start(), calls=%async_computation.7 | async-start | bytes 1081344 | tf_op jit(solution)/shard_map/all_gather | solution.py:121
  27.8 5.2 collective-permute-start.1
  33.0 0.6 copy-start.1
  35.5 14.5 %all-to-all-start.1 = ((bf16[64,2,2048]{2,0,1:T(8,128)(2,1)}), bf16[64,2,2048]{2,0,1:T(8,128)(2,1)S(1)}, u32[]{:S(2)}, u32[]{:S(2)}) async-start(bf16[64,2,2048]{2,0,1:T(8,128)(2,1)} %bitcast.89), calls=%async_computation.1 | async-start | bytes 1048576 | tf_op jit(solution)/shard_map/all_to_all | solution.py:74
  39.0 497.0 %all-gather.9.cloned.1.call-start = ((), (), s32[]{:S(2)}) async-start(), calls=%async_computation.6 | async-start | bytes 1081344 | tf_op jit(solution)/shard_map/all_gather | solution.py:120
  41.2 5.2 collective-permute-start
  46.4 0.6 copy-start.2
  538.4 1.9 copy-start
  547.9 1.9 copy-start
  557.3 1.9 copy-start
  566.8 1.9 copy-start
Sparse Core Ops, SparseCore 0:
  17.5 136.1 all-gather.4
  155.8 126.2 all-gather.6
  284.2 125.2 all-gather.10
  411.3 124.6 all-gather.8
where the time goes:
time: 596 us; the launch traced here: 594 us
  waiting for transfers between devices  403 us (68%)
  matrix products  72 us (12%)
  other arithmetic  33.8 us (6%)
  local copies, waits for them, and re-layouts  33.3 us (6%)
  blocking collectives  30.5 us (5%)
  between operations  13.3 us (2%)
  starting transfers between devices  7.43 us (1%)
    all_gather x1, waiting for transfers between devices, body(): value_block = lax.all_gather(local_value, 'inner', axis=0, tiled=True)  128 us
    all_gather x1, waiting for transfers between devices, body(): key_block = lax.all_gather(earlier_key, 'inner', axis=0, tiled=True)  127 us
    all_gather x1, waiting for transfers between devices, body(): key_block = lax.all_gather(local_key, 'inner', axis=0, tiled=True)  103 us
    dot_general x12, matrix products, fold_block(): jnp.einsum('kgrn,nkd->kgrd', weights.astype(jnp.bfloat16), value_heads, p...  46.5 us
    all_gather x1, waiting for transfers between devices, body(): value_block = lax.all_gather(earlier_value, 'inner', axis=0, tiled=True)  34.9 us
    reduce_sum x12, other arithmetic, fold_block(): new_total = run_total * factor + jnp.sum(weights, axis=-1)  29.5 us
    dot_general x12, matrix products, fold_block(): jnp.einsum('rkgd,nkd->kgrn', query_heads, key_heads, preferred_element_ty...  25.5 us
    dynamic_slice x48, local copies, waits for them, and re-layouts, fold_keys(): lax.scan(one_block, running, (key_block.reshape(steps, width_block, colum...  16.4 us
  transfers between devices with their start and end apart: 7, of which 7 were waited for; matrix products, arithmetic and copies ran while one was open for 16% of the time, Pallas kernels for 0%

commit v1 on v0

v1 whole, which is shorter than its diff:
```python
import functools
import math

import jax
import jax.numpy as jnp
from jax import lax
from jax.experimental import pallas as pl
from jax.experimental.pallas import tpu as pltpu
from jax.sharding import Mesh
from jax.sharding import PartitionSpec as P

HD = 128
TOK = 64
KVH = 4
GROUP = 8
ROWS = GROUP * TOK
CHUNK = 256
PER_CHUNK = CHUNK // TOK
LOW = -1e30
SCALE = math.log2(math.e) / math.sqrt(HD)

AXES = ("yh", "yl", "zh", "zp", "x", "c")
LINE = ("yh", "yl")
SHARE = ("yh", "yl", "zp")
RING = "zh"
STRETCHES = ("x", "c")
MIB = 1024 * 1024


def stacked_heads(q_ref, b):
    return jnp.concatenate(
        [q_ref[b, :, h * HD : (h + 1) * HD] for h in range(GROUP)], axis=0
    )


def fold(query, keys, values_t, visible, top_ref, total_ref, sum_ref, b):
    scores = lax.dot_general(
        keys, query, (((1,), (1,)), ((), ())), preferred_element_type=jnp.float32
    )
    if visible is not None:
        scores = jnp.where(visible, scores, LOW)
    old = top_ref[b]
    new = jnp.maximum(old, jnp.max(scores, axis=0, keepdims=True))
    weights = jnp.exp2((scores - new) * SCALE)
    factor = jnp.exp2((old - new) * SCALE)
    top_ref[b] = new
    total_ref[b] = total_ref[b] * factor + jnp.sum(weights, axis=0, keepdims=True)
    sum_ref[b] = sum_ref[b] * factor + jnp.dot(
        values_t, weights.astype(jnp.bfloat16), preferred_element_type=jnp.float32
    )


def earlier_kernel(info_ref, q_ref, kv_ref, top_ref, total_ref, sum_ref, k_s, vt_s):
    top_ref[...] = jnp.full(top_ref.shape, LOW, jnp.float32)
    total_ref[...] = jnp.zeros(total_ref.shape, jnp.float32)
    sum_ref[...] = jnp.zeros(sum_ref.shape, jnp.float32)
    chunks = vt_s.shape[0]

    @pl.when(info_ref[80] > 0)
    def _():
        flat = kv_ref[...].reshape(chunks * CHUNK, 2 * HD)
        for j in range(chunks):
            k_s[j] = flat[j * CHUNK : (j + 1) * CHUNK, :HD]
            vt_s[j] = flat[j * CHUNK : (j + 1) * CHUNK, HD:].T

        @pl.loop(0, q_ref.shape[0])
        def _(b):
            query = stacked_heads(q_ref, b)
            for j in range(chunks):
                fold(query, k_s[j], vt_s[j], None, top_ref, total_ref, sum_ref, b)


def own_kernel(
    info_ref, q_ref, kv_ref, top_in, total_in, sum_in, out_ref,
    top_ref, total_ref, sum_ref, k_s, v_s, vt_s,
):
    blocks = kv_ref.shape[0] * kv_ref.shape[1]
    across = kv_ref.shape[1]
    for i in range(blocks):
        at = pl.ds(pl.multiple_of(info_ref[i] * TOK, TOK), TOK)
        k_s[at, :] = kv_ref[i // across, i % across, :, :HD]
        v_s[at, :] = kv_ref[i // across, i % across, :, HD:]
    for j in range(vt_s.shape[0]):
        vt_s[j] = v_s[j * CHUNK : (j + 1) * CHUNK, :].T
    key_row = lax.broadcasted_iota(jnp.int32, (TOK, ROWS), 0)
    query_row = lax.broadcasted_iota(jnp.int32, (TOK, ROWS), 1) % TOK
    lead = query_row - key_row
    lane = lax.broadcasted_iota(jnp.int32, (TOK, HD), 1)

    @pl.loop(0, q_ref.shape[0])
    def _(b):
        top_ref[0] = top_in[b]
        total_ref[0] = total_in[b]
        sum_ref[0] = sum_in[b]
        query = stacked_heads(q_ref, b)
        own = info_ref[64 + b]
        seen = info_ref[72 + b]
        whole = info_ref[81 + b] // PER_CHUNK

        def keys_of(j):
            return k_s[pl.ds(pl.multiple_of(j * CHUNK, CHUNK), CHUNK), :]

        @pl.loop(0, whole)
        def _(j):
            fold(query, keys_of(j), vt_s[j], None, top_ref, total_ref, sum_ref, 0)

        @pl.when(seen > whole * PER_CHUNK)
        def _():
            visible = jnp.concatenate(
                [
                    lead >= (info_ref[32 + whole * PER_CHUNK + i] - own) * TOK
                    for i in range(PER_CHUNK)
                ],
                axis=0,
            )
            fold(query, keys_of(whole), vt_s[whole], visible, top_ref, total_ref, sum_ref, 0)

        total = total_ref[0]
        some = total > 0.0
        part = sum_ref[0] * jnp.where(some, 1.0 / jnp.where(some, total, 1.0), 0.0)
        part = part.T
        for h in range(GROUP):
            out_ref[b, :, h * HD : (h + 1) * HD] = part[h * TOK : (h + 1) * TOK].astype(
                jnp.bfloat16
            )
        level = jnp.where(some, top_ref[0] * SCALE + jnp.log2(jnp.where(some, total, 1.0)), LOW)
        level = jnp.broadcast_to(level, (HD, ROWS)).T
        picked = level[:TOK]
        for h in range(1, GROUP):
            picked = jnp.where(lane % GROUP == h, level[h * TOK : (h + 1) * TOK], picked)
        high = picked.astype(jnp.bfloat16).astype(jnp.float32)
        middle = (picked - high).astype(jnp.bfloat16).astype(jnp.float32)
        rest = picked - high - middle
        pieces = jnp.where(
            lane < GROUP,
            high,
            jnp.where(lane < 2 * GROUP, middle, jnp.where(lane < 3 * GROUP, rest, 0.0)),
        )
        out_ref[b, :, GROUP * HD :] = pieces.astype(jnp.bfloat16)


def join_kernel(parts_ref, out_ref):
    for m in range(KVH):
        level = []
        for p in range(2):
            pieces = parts_ref[2 * m + p, :, GROUP * HD :].astype(jnp.float32)
            level.append(
                pieces
                + pltpu.roll(pieces, HD - GROUP, 1)
                + pltpu.roll(pieces, HD - 2 * GROUP, 1)
            )
        share = 1.0 / (1.0 + jnp.exp2(level[1] - level[0]))
        for h in range(GROUP):
            first = parts_ref[2 * m, :, h * HD : (h + 1) * HD].astype(jnp.float32)
            second = parts_ref[2 * m + 1, :, h * HD : (h + 1) * HD].astype(jnp.float32)
            mixed = second + (first - second) * share[:, h : h + 1]
            at = (m * GROUP + h) * HD
            out_ref[:, at : at + HD] = mixed.astype(jnp.bfloat16)


def in_vmem():
    return pl.BlockSpec(memory_space=pltpu.VMEM)


def in_smem():
    return pl.BlockSpec(memory_space=pltpu.SMEM)


def tables(block_order):
    zh, zp = lax.axis_index("zh"), lax.axis_index("zp")
    stretch = lax.axis_index(STRETCHES)
    ids = lax.dynamic_index_in_dim(block_order, stretch, 2, keepdims=False)
    ids = ids.reshape(2, 2, lax.axis_size("zh"), lax.axis_size("zp"))
    keys = lax.dynamic_index_in_dim(ids, zp, 3, keepdims=False)
    keys = keys.transpose(2, 0, 1).reshape(-1)
    queries = lax.dynamic_index_in_dim(ids, zh, 2, keepdims=False).reshape(-1)
    place = jnp.sum(keys[None, :] < keys[:, None], axis=1, dtype=jnp.int32)
    slots = jnp.arange(keys.shape[0], dtype=jnp.int32)
    in_order = jnp.sum(jnp.where(place[None, :] == slots[:, None], keys[None, :], 0), axis=1)
    seen = jnp.sum(keys[None, :] <= queries[:, None], axis=1, dtype=jnp.int32)
    before = jnp.sum(keys[None, :] < queries[:, None], axis=1, dtype=jnp.int32)
    return jnp.concatenate([place, in_order, queries, seen, stretch.reshape(1), before])


def body(queries, keys, values, block_order):
    tokens = queries.shape[0]
    lines = KVH
    kv = jnp.stack(
        [
            jnp.concatenate(
                [keys[:, m * HD : (m + 1) * HD], values[:, m * HD : (m + 1) * HD]], axis=1
            )
            for m in range(lines)
        ]
    )
    own = lax.all_to_all(kv, LINE, split_axis=0, concat_axis=0, tiled=True)
    count = lax.axis_size("x") * lax.axis_size("c")
    earlier = lax.ppermute(own[2:], STRETCHES, [(i, i + 1) for i in range(count - 1)])
    own_all = lax.all_gather(own, RING, axis=0)
    earlier_all = lax.all_gather(earlier, RING, axis=0)
    info = tables(block_order)

    width = GROUP * HD
    split = queries.reshape(tokens, lines, width).transpose(1, 0, 2)
    pairs = lax.axis_size("zp")
    split = jnp.broadcast_to(split[:, None], (lines, pairs, tokens, width))
    split = split.reshape(lines * pairs, tokens, width)
    query = lax.all_to_all(split, SHARE, split_axis=0, concat_axis=0, tiled=True)
    blocks = lines * pairs

    rings = lax.axis_size(RING)
    chunks = rings * 2 * TOK // CHUNK
    state = [
        jax.ShapeDtypeStruct((blocks, 1, ROWS), jnp.float32),
        jax.ShapeDtypeStruct((blocks, 1, ROWS), jnp.float32),
        jax.ShapeDtypeStruct((blocks, HD, ROWS), jnp.float32),
    ]
    with jax.named_scope("earlier_part"):
        top, total, summed = pl.pallas_call(
            earlier_kernel,
            out_shape=state,
            in_specs=[in_smem(), in_vmem(), in_vmem()],
            out_specs=[in_vmem()] * 3,
            scratch_shapes=[
                pltpu.VMEM((chunks, CHUNK, HD), jnp.bfloat16),
                pltpu.VMEM((chunks, HD, CHUNK), jnp.bfloat16),
            ],
            compiler_params=pltpu.CompilerParams(vmem_limit_bytes=32 * MIB),
            cost_estimate=pl.CostEstimate(
                flops=4 * blocks * ROWS * chunks * CHUNK * HD,
                bytes_accessed=4 * MIB,
                transcendentals=blocks * ROWS * chunks * CHUNK,
            ),
        )(info, query, earlier_all)
    with jax.named_scope("own_part"):
        part = pl.pallas_call(
            own_kernel,
            out_shape=jax.ShapeDtypeStruct((blocks, tokens, width + HD), jnp.bfloat16),
            in_specs=[in_smem()] + [in_vmem()] * 5,
            out_specs=in_vmem(),
            scratch_shapes=[
                pltpu.VMEM((1, 1, ROWS), jnp.float32),
                pltpu.VMEM((1, 1, ROWS), jnp.float32),
                pltpu.VMEM((1, HD, ROWS), jnp.float32),
                pltpu.VMEM((2 * chunks * CHUNK, HD), jnp.bfloat16),
                pltpu.VMEM((2 * chunks * CHUNK, HD), jnp.bfloat16),
                pltpu.VMEM((2 * chunks, HD, CHUNK), jnp.bfloat16),
            ],
            compiler_params=pltpu.CompilerParams(vmem_limit_bytes=32 * MIB),
            cost_estimate=pl.CostEstimate(
                flops=4 * blocks * ROWS * chunks * CHUNK * HD,
                bytes_accessed=6 * MIB,
                transcendentals=blocks * ROWS * chunks * CHUNK,
            ),
        )(info, query, own_all, top, total, summed)
    parts = lax.all_to_all(part, SHARE, split_axis=0, concat_axis=0, tiled=True)
    with jax.named_scope("join_parts"):
        return pl.pallas_call(
            join_kernel,
            out_shape=jax.ShapeDtypeStruct((tokens, lines * width), jnp.bfloat16),
            in_specs=[in_vmem()],
            out_specs=in_vmem(),
            compiler_params=pltpu.CompilerParams(vmem_limit_bytes=32 * MIB),
            cost_estimate=pl.CostEstimate(
                flops=3 * tokens * lines * width, bytes_accessed=2 * MIB, transcendentals=0
            ),
        )(parts)


def solution(mesh):
    fine = Mesh(mesh.devices.reshape(2, 2, 8, 2, 4, 2), AXES)
    rows = P(AXES, None)
    return jax.shard_map(
        body, mesh=fine, in_specs=(rows, rows, rows, P()), out_specs=rows, check_vma=False
    )
```

time: 596 us -> 141 us (0.24)
  the two profiles are of different devices: /device:TPU:2 before, /device:TPU:4 now
where the time goes in v1:
time: 141 us; the launch traced here: 140 us
  blocking collectives  62.4 us (44%)
  Pallas kernels  34.3 us (24%)
  between operations  13.5 us (10%)
  starting transfers between devices  10.2 us (7%)
  waiting for transfers between devices  9.57 us (7%)
  local copies, waits for them, and re-layouts  9 us (6%)
    all_gather x1, blocking collectives, body(): earlier_all = lax.all_gather(earlier, RING, axis=0)  43.3 us
    pallas_call x1, Pallas kernels, body(): pl.pallas_call(own_kernel, out_shape=jax.ShapeDtypeStruct((blocks, tokens...  19.8 us
    all_to_all x1, blocking collectives, body(): parts = lax.all_to_all(part, SHARE, split_axis=0, concat_axis=0, tiled=True)  19.1 us
    pallas_call x1, Pallas kernels, body(): pl.pallas_call(earlier_kernel, out_shape=state, in_specs=[in_smem(), in_v...  12.8 us
    all_to_all x1, waiting for transfers between devices, body(): own = lax.all_to_all(kv, LINE, split_axis=0, concat_axis=0, tiled=True)  5.43 us
    all_to_all x1, starting transfers between devices, body(): own = lax.all_to_all(kv, LINE, split_axis=0, concat_axis=0, tiled=True)  4.46 us
    unnamed x12, local copies, waits for them, and re-layouts  4.17 us
    all_to_all x1, starting transfers between devices, body(): lax.all_to_all(split, SHARE, split_axis=0, concat_axis=0, tiled=True)  3.8 us
  transfers between devices with their start and end apart: 4, of which 2 were waited for; matrix products, arithmetic and copies ran while one was open for 2% of the time, Pallas kernels for 9%

profile of v1, /device:TPU:4, one launch (start us, length us, event | category | flops | bytes accessed | tf_op | source)
XLA Modules:
  0.0 140.1 jit_solution(8672728666900494948)
XLA Ops:
  6.5 0.0 copy-start
  6.5 0.0 copy-start.5
  6.5 0.8 fusion
  7.4 0.8 fusion.1
  8.2 0.7 pad_maximum_fusion
  8.9 4.5 %all-to-all-start.1 = ((bf16[4,64,256]{2,1,0:T(8,128)(2,1)}), bf16[4,64,256]{2,1,0:T(8,128)(2,1)S(1)}, u32[]{:S(2)}, u32[]{:S(2)}) async-start(bf16[4,64,256]{2,1,0:T(8,128)(2,1)} %pad_maximum_fusion), calls=%async_computation.1 | async-start | bytes 262144 | tf_op jit(solution)/shard_map/all_to_all | solution.py:196
  13.3 0.0 copy-done.5
  13.3 0.4 reshape.26
  13.7 0.2 copy.12
  13.9 5.4 %all-to-all-done.1 = bf16[4,64,256]{2,1,0:T(8,128)(2,1)S(1)} async-done(((bf16[4,64,256]{2,1,0:T(8,128)(2,1)}), bf16[4,64,256]{2,1,0:T(8,128)(2,1)S(1)}, u32[]{:S(2)}, u32[]{:S(2)}) %all-to-all-start.1) | async-done | bytes 131104 | tf_op jit(solution)/shard_map/all_to_all | solution.py:196
  19.3 0.0 copy-start.4
  19.3 1.1 broadcast_in_dim.13
  20.4 0.0 copy-done.4
  20.4 3.8 %all-to-all-start = ((bf16[8,64,1024]{2,1,0:T(8,128)(2,1)}), bf16[8,64,1024]{2,1,0:T(8,128)(2,1)S(1)}, u32[]{:S(2)}, u32[]{:S(2)}) async-start(bf16[8,64,1024]{2,1,0:T(8,128)(2,1)} %bitcast.3), calls=%async_computation | async-start | bytes 2097152 | tf_op jit(solution)/shard_map/all_to_all | solution.py:208
  24.2 0.0 all-gather.4.cloned.1.call-start
  24.3 0.7 all-gather.4.cloned.1.call-update
  25.0 0.0 copy-done
  25.0 0.1 reshape.23
  25.1 0.1 reshape.24
  25.2 0.2 dynamic-slice_reduce_fusion
  25.4 0.1 copy.11
  25.5 0.1 lt.38
  25.6 0.2 convert_reduce_fusion
  25.8 0.2 convert_reduce_fusion.1
  26.0 0.9 slice.36
  26.8 1.9 %collective-permute-start = (bf16[2,64,256]{2,1,0:T(8,128)(2,1)S(1)}, bf16[2,64,256]{2,1,0:T(8,128)(2,1)S(1)}, u32[]{:S(2)}, u32[]{:S(2)}) collective-permute-start(bf16[2,64,256]{2,1,0:T(8,128)(2,1)S(1)} %slice.36), channel_id=1, source_target_pairs={{0,1},{1,2},{2,3},{3,4},{4,5},{5,6},{6,7},{8,9},{9,10},{10,11},{11... | collective-permute-start | bytes 196616 | tf_op jit(solution)/shard_map/ppermute | solution.py:198
  28.7 0.1 select_reduce_fusion
  28.9 0.1 concatenate.15.info_ref
  28.9 3.5 %collective-permute-done = bf16[2,64,256]{2,1,0:T(8,128)(2,1)S(1)} collective-permute-done((bf16[2,64,256]{2,1,0:T(8,128)(2,1)S(1)}, bf16[2,64,256]{2,1,0:T(8,128)(2,1)S(1)}, u32[]{:S(2)}, u32[]{:S(2)}) %collective-permute-start) | collective-permute-done | bytes 65568 | tf_op jit(solution)/shard_map/ppermute | solution.py:198
  32.4 43.3 %all-gather.1 = bf16[16,64,256]{2,1,0:T(8,128)(2,1)S(1)} all-gather(bf16[2,64,256]{2,1,0:T(8,128)(2,1)S(1)} %collective-permute-done), channel_id=3, replica_groups=mesh['yh'=2,'yl'=2,'zh'=8,'zp'=2,'x'=4,'c'=2] {'zh'}, dimensions={0}, use_global_device_ids=true | all-gather | bytes 589824 | tf_op jit(solution)/shard_map/all_gather | solution.py:200
  75.7 0.0 all-to-all-done.q_ref
  75.7 12.8 %earlier_part.1 = (f32[8,1,512]{2,1,0:T(1,128)S(1)}, f32[8,1,512]{2,1,0:T(1,128)S(1)}, f32[8,128,512]{2,1,0:T(8,128)S(1)}) custom-call(s32[89]{0:T(128)S(1)} %concatenate.15.info_ref, bf16[8,64,1024]{2,1,0:T(8,128)(2,1)S(1)} %all-to-all-done.q_ref, bf16[8,2,64,256]{3,2,1,0:T(8,128)(2,1)S(1)} %bitcast.14), custom_call_target="tpu_custom_call" | custom-call | flops 2147483648 | bytes 4194304 | tf_op jit(solution)/shard_map/earlier_part/pallas_call | solution.py:219
  88.5 0.0 copy-start.2
  88.5 1.3 copy-done.2
  89.8 0.0 all-gather.4.cloned.1.call-done
  89.9 0.0 copy-start.1
  89.9 1.2 copy-done.1
  91.1 0.0 copy-start.3
  91.1 1.6 %copy-done.3 = f32[8,128,512]{2,1,0:T(8,128)S(1)} copy-done((f32[8,128,512]{2,1,0:T(8,128)S(1)}, f32[8,128,512]{2,1,0:T(8,128)}, u32[]{:S(2)}) %copy-start.3) | copy-done | bytes 2097176
  92.7 19.8 %own_part.1 = bf16[8,64,1152]{2,1,0:T(8,128)(2,1)S(1)} custom-call(s32[89]{0:T(128)S(1)} %concatenate.15.info_ref, bf16[8,64,1024]{2,1,0:T(8,128)(2,1)S(1)} %all-to-all-done.q_ref, bf16[8,4,64,256]{3,2,1,0:T(8,128)(2,1)S(1)} %bitcast.15, f32[8,1,512]{2,1,0:T(1,128)S(1)} %get-tuple-element.8.top_in, f32[8,1,512]{2,1,0:T(1,128)S(1)} %get-tuple-element.9.total_in, ...), custom_call_target="tpu_custom_call" | custom-call | flops 2147483648 | bytes 6291456 | tf_op jit(solution)/shard_map/own_part/pallas_call | solution.py:236
  112.5 19.1 %all_to_all.15.parts_ref = bf16[8,64,1152]{2,1,0:T(8,128)(2,1)S(1)} all-to-all(bf16[8,64,1152]{2,1,0:T(8,128)(2,1)S(1)} %own_part.1), channel_id=1, replica_groups=mesh['yh'=2,'yl'=2,'zh'=8,'zp'=2,'x'=4,'c'=2] {'yh','yl','zp'}, dimensions={0} | all-to-all | bytes 2359296 | tf_op jit(solution)/shard_map/all_to_all | solution.py:256
  131.6 1.7 %join_parts.1 = bf16[64,4096]{1,0:T(8,128)(2,1)} custom-call(bf16[8,64,1152]{2,1,0:T(8,128)(2,1)S(1)} %all_to_all.15.parts_ref), custom_call_target="tpu_custom_call" | custom-call | flops 786432 | bytes 2097152 | tf_op jit(solution)/shard_map/join_parts/pallas_call | solution.py:258
  (4 shorter events, 0.1 us)
Async XLA Ops:
  6.5 18.4 %copy-start = (s32[2,32,8]{1,2,0:T(8,128)S(1)}, s32[2,32,8]{1,2,0:T(8,128)}, u32[]{:S(2)}) copy-start(s32[2,32,8]{1,2,0:T(8,128)} %param.7) | copy-start | bytes 6148
  6.5 6.8 %copy-start.5 = (bf16[64,4096]{1,0:T(8,128)(2,1)S(1)}, bf16[64,4096]{1,0:T(8,128)(2,1)}, u32[]{:S(2)}) copy-start(bf16[64,4096]{1,0:T(8,128)(2,1)} %param.4) | copy-start | bytes 1572868
  8.9 10.4 %all-to-all-start.1 = ((bf16[4,64,256]{2,1,0:T(8,128)(2,1)}), bf16[4,64,256]{2,1,0:T(8,128)(2,1)S(1)}, u32[]{:S(2)}, u32[]{:S(2)}) async-start(bf16[4,64,256]{2,1,0:T(8,128)(2,1)} %pad_maximum_fusion), calls=%async_computation.1 | async-start | bytes 262144 | tf_op jit(solution)/shard_map/all_to_all | solution.py:196
  19.3 1.1 copy-start.4
  20.4 55.3 %all-to-all-start = ((bf16[8,64,1024]{2,1,0:T(8,128)(2,1)}), bf16[8,64,1024]{2,1,0:T(8,128)(2,1)S(1)}, u32[]{:S(2)}, u32[]{:S(2)}) async-start(bf16[8,64,1024]{2,1,0:T(8,128)(2,1)} %bitcast.3), calls=%async_computation | async-start | bytes 2097152 | tf_op jit(solution)/shard_map/all_to_all | solution.py:208
  24.2 65.6 %all-gather.4.cloned.1.call-start = ((), (), s32[]{:S(2)}) async-start(), calls=%async_computation.3 | async-start | bytes 1179648 | tf_op jit(solution)/shard_map/all_gather | solution.py:199
  26.8 5.6 %collective-permute-start = (bf16[2,64,256]{2,1,0:T(8,128)(2,1)S(1)}, bf16[2,64,256]{2,1,0:T(8,128)(2,1)S(1)}, u32[]{:S(2)}, u32[]{:S(2)}) collective-permute-start(bf16[2,64,256]{2,1,0:T(8,128)(2,1)S(1)} %slice.36), channel_id=1, source_target_pairs={{0,1},{1,2},{2,3},{3,4},{4,5},{5,6},{6,7},{8,9},{9,10},{10,11},{11... | collective-permute-start | bytes 196616 | tf_op jit(solution)/shard_map/ppermute | solution.py:198
  88.5 1.4 copy-start.2
  89.9 1.2 copy-start.1
  91.1 1.6 %copy-start.3 = (f32[8,128,512]{2,1,0:T(8,128)S(1)}, f32[8,128,512]{2,1,0:T(8,128)}, u32[]{:S(2)}) copy-start(f32[8,128,512]{2,1,0:T(8,128)} %copy-done.2) | copy-start | bytes 6291460
Sparse Core Ops, SparseCore 0:
  27.1 59.9 all-gather.3

commit v2 on v1

v2 whole, which is shorter than its diff:
```python
import functools
import math

import jax
import jax.numpy as jnp
from jax import lax
from jax.experimental import pallas as pl
from jax.experimental.pallas import tpu as pltpu
from jax.sharding import Mesh
from jax.sharding import PartitionSpec as P

HD = 128
TOK = 64
KVH = 4
GROUP = 8
ROWS = GROUP * TOK
CHUNK = 256
PER_CHUNK = CHUNK // TOK
LOW = -1e30
SCALE = math.log2(math.e) / math.sqrt(HD)

AXES = ("yh", "yl", "za", "zb", "zp", "x", "c")
LINE = ("yh", "yl")
SHARE = ("yh", "yl", "zp")
FAR = "za"
RING = ("za", "zb")
STRETCHES = ("x", "c")
ONWARD = ("za", "zb", "x", "c")
MIB = 1024 * 1024
ONES = 16
SIDE = HD + ONES


def stacked_heads(q_ref, b):
    return jnp.concatenate(
        [q_ref[b, :, h * HD : (h + 1) * HD] for h in range(GROUP)], axis=0
    )


def score(keys, query):
    return lax.dot_general(
        keys, query, (((1,), (1,)), ((), ())), preferred_element_type=jnp.float32
    )


def weigh(values_t, scores, top):
    weights = jnp.exp2((scores - top) * SCALE).astype(jnp.bfloat16)
    return jnp.dot(values_t, weights, preferred_element_type=jnp.float32)


def own_kernel(
    info_ref, q_ref, far_ref, next_ref, prev_ref, top_ref, total_ref, sum_ref,
    k_s, v_s, vt_s, lead_s, score_s, top_s, piece_s, piece_top,
):
    across = far_ref.shape[1]
    split = next_ref.shape[0]
    half = far_ref.shape[0] * across
    for i in range(2 * half):
        ring, line = (i % half) // across, i % across
        if i < half:
            block = far_ref[ring, line]
        elif ring < split:
            block = next_ref[ring, line]
        else:
            block = prev_ref[ring - split, line]
        at = pl.ds(pl.multiple_of(info_ref[i] * TOK, TOK), TOK)
        k_s[at, :] = block[:, :HD]
        v_s[at, :] = block[:, HD:]
    count = k_s.shape[0]
    for j in range(0, count, CHUNK):
        vt_s[:HD, j : j + CHUNK] = v_s[j : j + CHUNK, :].T
    vt_s[HD:, :] = jnp.ones((ONES, count), jnp.bfloat16)
    key_row = lax.broadcasted_iota(jnp.int32, (TOK, ROWS), 0)
    query_row = lax.broadcasted_iota(jnp.int32, (TOK, ROWS), 1) % TOK
    lead_s[...] = query_row - key_row
    pairs = q_ref.shape[0] // 2
    lower = count // 2
    top_ref[:pairs] = jnp.full((pairs, 1, ROWS), LOW, jnp.float32)
    total_ref[:pairs] = jnp.zeros((pairs, 1, ROWS), jnp.float32)
    sum_ref[:pairs] = jnp.zeros((pairs, HD, ROWS), jnp.float32)

    def begin(b, slot):
        scores = score(k_s[:lower, :], stacked_heads(q_ref, b))
        score_s[slot] = scores
        top_s[slot] = jnp.max(scores, axis=0, keepdims=True)

    def end(b, slot):
        top = top_s[slot]
        both = weigh(vt_s[:, :lower], score_s[slot], top)
        top_ref[b] = top
        total_ref[b] = both[HD : HD + 1]
        sum_ref[b] = both[:HD]

    begin(pairs, 0)

    @pl.loop(0, pairs // 2)
    def _(i):
        b = pairs + 2 * i
        begin(b + 1, 1)
        end(b, 0)
        begin(jnp.minimum(b + 2, 2 * pairs - 1), 0)
        end(b + 1, 1)

    steps = lower // CHUNK + 1
    items = pairs * steps

    def place(item):
        pair, step = item // steps, item % steps
        low = (info_ref[72 + pair] + PER_CHUNK - 1) // PER_CHUNK
        high = (info_ref[72 + pairs + pair] - lower // TOK + PER_CHUNK - 1) // PER_CHUNK
        is_low = step < low
        b = jnp.where(is_low, pair, pairs + pair)
        chunk = jnp.where(is_low, step, jnp.minimum(steps - 1 + step - low, 2 * steps - 3))
        own = jnp.where(step < low + high, info_ref[64 + b], -4096)
        return b, chunk, own

    def begin_item(item, slot):
        b, chunk, own = place(item)
        at = pl.ds(pl.multiple_of(chunk * CHUNK, CHUNK), CHUNK)
        scores = score(k_s[at, :], stacked_heads(q_ref, b))
        top = None
        for i in range(PER_CHUNK):
            ahead = (info_ref[32 + chunk * PER_CHUNK + i] - own) * TOK
            part = scores[i * TOK : (i + 1) * TOK]
            part = jnp.where(lead_s[...] >= ahead, part, LOW)
            piece_s[slot, i * TOK : (i + 1) * TOK, :] = part
            high = jnp.max(part, axis=0, keepdims=True)
            top = high if top is None else jnp.maximum(top, high)
        piece_top[slot] = top

    def end_item(item, slot):
        b, chunk, own = place(item)
        at = pl.ds(pl.multiple_of(chunk * CHUNK, CHUNK), CHUNK)
        old = top_ref[b]
        top = jnp.maximum(old, piece_top[slot])
        both = weigh(vt_s[:, at], piece_s[slot], top)
        factor = jnp.exp2((old - top) * SCALE)
        top_ref[b] = top
        total_ref[b] = total_ref[b] * factor + both[HD : HD + 1]
        sum_ref[b] = sum_ref[b] * factor + both[:HD]

    begin_item(0, 0)

    @pl.loop(0, items // 2)
    def _(i):
        begin_item(2 * i + 1, 1)
        end_item(2 * i, 0)
        begin_item(jnp.minimum(2 * i + 2, items - 1), 0)
        end_item(2 * i + 1, 1)


def earlier_kernel(
    info_ref, q_ref, far_ref, next_ref, prev_ref, top_in, total_in, sum_in, out_ref,
    k_s, vt_s, score_s, top_s,
):
    lane = lax.broadcasted_iota(jnp.int32, (TOK, HD), 1)

    def finish(b, top, total, summed):
        some = total > 0.0
        safe = jnp.where(some, total, 1.0)
        part = (summed * (1.0 / safe)).T
        for h in range(GROUP):
            out_ref[b, :, h * HD : (h + 1) * HD] = part[h * TOK : (h + 1) * TOK].astype(
                jnp.bfloat16
            )
        level = jnp.where(some, top * SCALE + jnp.log2(safe), LOW)
        level = jnp.broadcast_to(level, (HD, ROWS)).T
        picked = level[:TOK]
        for h in range(1, GROUP):
            picked = jnp.where(lane % GROUP == h, level[h * TOK : (h + 1) * TOK], picked)
        high = picked.astype(jnp.bfloat16).astype(jnp.float32)
        middle = (picked - high).astype(jnp.bfloat16).astype(jnp.float32)
        rest = picked - high - middle
        pieces = jnp.where(
            lane < GROUP,
            high,
            jnp.where(lane < 2 * GROUP, middle, jnp.where(lane < 3 * GROUP, rest, 0.0)),
        )
        out_ref[b, :, GROUP * HD :] = pieces.astype(jnp.bfloat16)

    blocks = q_ref.shape[0]

    @pl.when(info_ref[80] == 0)
    def _():
        @pl.loop(0, blocks)
        def _(b):
            finish(b, top_in[b], total_in[b], sum_in[b])

    @pl.when(info_ref[80] > 0)
    def _():
        at = 0
        for ref in (far_ref, next_ref, prev_ref):
            rows = ref.shape[0] * ref.shape[1] * TOK
            flat = ref[...].reshape(rows, 2 * HD)
            k_s[at : at + rows, :] = flat[:, :HD]
            for j in range(0, rows, CHUNK):
                vt_s[:HD, at + j : at + j + CHUNK] = flat[j : j + CHUNK, HD:].T
            at += rows
        vt_s[HD:, :] = jnp.ones((ONES, at), jnp.bfloat16)

        def begin(b, slot):
            scores = score(k_s[...], stacked_heads(q_ref, b))
            score_s[slot] = scores
            top_s[slot] = jnp.max(scores, axis=0, keepdims=True)

        def end(b, slot):
            old = top_in[b]
            top = jnp.maximum(old, top_s[slot])
            both = weigh(vt_s[...], score_s[slot], top)
            factor = jnp.exp2((old - top) * SCALE)
            finish(
                b,
                top,
                total_in[b] * factor + both[HD : HD + 1],
                sum_in[b] * factor + both[:HD],
            )

        begin(0, 0)

        @pl.loop(0, blocks // 2)
        def _(i):
            begin(2 * i + 1, 1)
            end(2 * i, 0)
            begin(jnp.minimum(2 * i + 2, blocks - 1), 0)
            end(2 * i + 1, 1)


def join_kernel(parts_ref, out_ref):
    for m in range(KVH):
        level = []
        for p in range(2):
            pieces = parts_ref[2 * m + p, :, GROUP * HD :].astype(jnp.float32)
            level.append(
                pieces
                + pltpu.roll(pieces, HD - GROUP, 1)
                + pltpu.roll(pieces, HD - 2 * GROUP, 1)
            )
        share = 1.0 / (1.0 + jnp.exp2(level[1] - level[0]))
        for h in range(GROUP):
            first = parts_ref[2 * m, :, h * HD : (h + 1) * HD].astype(jnp.float32)
            second = parts_ref[2 * m + 1, :, h * HD : (h + 1) * HD].astype(jnp.float32)
            mixed = second + (first - second) * share[:, h : h + 1]
            at = (m * GROUP + h) * HD
            out_ref[:, at : at + HD] = mixed.astype(jnp.bfloat16)


def in_vmem():
    return pl.BlockSpec(memory_space=pltpu.VMEM)


def in_smem():
    return pl.BlockSpec(memory_space=pltpu.SMEM)


def tables(block_order):
    za, zb, zp = (lax.axis_index(name) for name in ("za", "zb", "zp"))
    stretch = lax.axis_index(STRETCHES)
    ids = lax.dynamic_index_in_dim(block_order, stretch, 2, keepdims=False)
    ids = ids.reshape(2, 2, lax.axis_size("za"), lax.axis_size("zb"), lax.axis_size("zp"))
    keys = lax.dynamic_index_in_dim(ids, zp, 4, keepdims=False)
    near = lax.dynamic_index_in_dim(keys, zb, 3, keepdims=False)
    other = lax.dynamic_index_in_dim(keys, 1 - zb, 3, keepdims=False)
    keys = jnp.stack([near, other]).transpose(0, 3, 1, 2).reshape(-1)
    queries = lax.dynamic_index_in_dim(ids, za, 2, keepdims=False)
    queries = lax.dynamic_index_in_dim(queries, zb, 2, keepdims=False).reshape(-1)
    place = jnp.sum(keys[None, :] < keys[:, None], axis=1, dtype=jnp.int32)
    slots = jnp.arange(keys.shape[0], dtype=jnp.int32)
    in_order = jnp.sum(jnp.where(place[None, :] == slots[:, None], keys[None, :], 0), axis=1)
    seen = jnp.sum(keys[None, :] <= queries[:, None], axis=1, dtype=jnp.int32)
    return jnp.concatenate([place, in_order, queries, seen, stretch.reshape(1)])


def onward(block, step, stretches):
    ring = lax.axis_size(RING)
    outer = lax.axis_size(STRETCHES)
    route = [
        (r * outer + o, (r + step) % ring * outer + o + stretches)
        for r in range(ring)
        for o in range(outer - stretches)
    ]
    return lax.ppermute(block, ONWARD, route)


def body(queries, keys, values, block_order):
    tokens = queries.shape[0]
    lines = KVH
    kv = jnp.stack(
        [
            jnp.concatenate(
                [keys[:, m * HD : (m + 1) * HD], values[:, m * HD : (m + 1) * HD]], axis=1
            )
            for m in range(lines)
        ]
    )
    own = lax.all_to_all(kv, LINE, split_axis=0, concat_axis=0, tiled=True)
    far = lax.all_gather(own, FAR, axis=0)
    cut = far.shape[0] // 2
    upper = far[:, 2:]
    own_next = onward(far[:cut], -1, 0)
    own_prev = onward(far[cut:], 1, 0)
    earlier_far = onward(upper, 0, 1)
    earlier_next = onward(upper[:cut], -1, 1)
    earlier_prev = onward(upper[cut:], 1, 1)
    info = tables(block_order)

    width = GROUP * HD
    split = queries.reshape(tokens, lines, width).transpose(1, 0, 2)
    pairs = lax.axis_size("zp")
    split = jnp.broadcast_to(split[:, None], (lines, pairs, tokens, width))
    split = split.reshape(lines * pairs, tokens, width)
    query = lax.all_to_all(split, SHARE, split_axis=0, concat_axis=0, tiled=True)
    blocks = lines * pairs

    count = lax.axis_size(RING) * 2 * TOK
    state = [
        jax.ShapeDtypeStruct((blocks, 1, ROWS), jnp.float32),
        jax.ShapeDtypeStruct((blocks, 1, ROWS), jnp.float32),
        jax.ShapeDtypeStruct((blocks, HD, ROWS), jnp.float32),
    ]
    params = pltpu.CompilerParams(vmem_limit_bytes=40 * MIB)
    cost = pl.CostEstimate(
        flops=4 * blocks * ROWS * count * HD,
        bytes_accessed=4 * MIB,
        transcendentals=blocks * ROWS * count,
    )
    slots = [
        pltpu.VMEM((2, count, ROWS), jnp.float32),
        pltpu.VMEM((2, 1, ROWS), jnp.float32),
    ]
    with jax.named_scope("own_part"):
        top, total, summed = pl.pallas_call(
            own_kernel,
            out_shape=state,
            in_specs=[in_smem()] + [in_vmem()] * 4,
            out_specs=[in_vmem()] * 3,
            scratch_shapes=[
                pltpu.VMEM((2 * count, HD), jnp.bfloat16),
                pltpu.VMEM((2 * count, HD), jnp.bfloat16),
                pltpu.VMEM((SIDE, 2 * count), jnp.bfloat16),
                pltpu.VMEM((TOK, ROWS), jnp.int32),
                *slots,
                pltpu.VMEM((2, CHUNK, ROWS), jnp.float32),
                pltpu.VMEM((2, 1, ROWS), jnp.float32),
            ],
            compiler_params=params,
            cost_estimate=cost,
        )(info, query, far, own_next, own_prev)
    with jax.named_scope("earlier_part"):
        part = pl.pallas_call(
            earlier_kernel,
            out_shape=jax.ShapeDtypeStruct((blocks, tokens, width + HD), jnp.bfloat16),
            in_specs=[in_smem()] + [in_vmem()] * 7,
            out_specs=in_vmem(),
            scratch_shapes=[
                pltpu.VMEM((count, HD), jnp.bfloat16),
                pltpu.VMEM((SIDE, count), jnp.bfloat16),
                *slots,
            ],
            compiler_params=params,
            cost_estimate=cost,
        )(info, query, earlier_far, earlier_next, earlier_prev, top, total, summed)
    parts = lax.all_to_all(part, SHARE, split_axis=0, concat_axis=0, tiled=True)
    with jax.named_scope("join_parts"):
        return pl.pallas_call(
            join_kernel,
            out_shape=jax.ShapeDtypeStruct((tokens, lines * width), jnp.bfloat16),
            in_specs=[in_vmem()],
            out_specs=in_vmem(),
            compiler_params=params,
            cost_estimate=pl.CostEstimate(
                flops=3 * tokens * lines * width, bytes_accessed=2 * MIB, transcendentals=0
            ),
        )(parts)


def solution(mesh):
    fine = Mesh(mesh.devices.reshape(2, 2, 4, 2, 2, 4, 2), AXES)
    rows = P(AXES, None)
    return jax.shard_map(
        body, mesh=fine, in_specs=(rows, rows, rows, P()), out_specs=rows, check_vma=False
    )
```

time: 141 us -> 120 us (0.85)
  the two profiles are of different devices: /device:TPU:4 before, /device:TPU:2 now
where the time goes in v2:
time: 120 us; the launch traced here: 119 us
  blocking collectives  62.1 us (52%)
  starting transfers between devices  26.8 us (22%)
  Pallas kernels  18.2 us (15%)
  waiting for transfers between devices  5.45 us (5%)
  local copies, waits for them, and re-layouts  5.27 us (4%)
    all_gather x1, blocking collectives, body(): far = lax.all_gather(own, FAR, axis=0)  37.9 us
    all_to_all x1, blocking collectives, body(): parts = lax.all_to_all(part, SHARE, split_axis=0, concat_axis=0, tiled=True)  24.3 us
    ppermute x5, starting transfers between devices, onward(): return lax.ppermute(block, ONWARD, route)  18.5 us
    pallas_call x1, Pallas kernels, body(): pl.pallas_call(own_kernel, out_shape=state, in_specs=[in_smem()] + [in_vm...  9.81 us
    pallas_call x1, Pallas kernels, body(): pl.pallas_call(earlier_kernel, out_shape=jax.ShapeDtypeStruct((blocks, to...  6.66 us
    all_to_all x1, waiting for transfers between devices, body(): own = lax.all_to_all(kv, LINE, split_axis=0, concat_axis=0, tiled=True)  5.43 us
    all_to_all x1, starting transfers between devices, body(): own = lax.all_to_all(kv, LINE, split_axis=0, concat_axis=0, tiled=True)  4.46 us
    all_to_all x1, starting transfers between devices, body(): lax.all_to_all(split, SHARE, split_axis=0, concat_axis=0, tiled=True)  3.8 us
  transfers between devices with their start and end apart: 7, of which 1 were waited for; matrix products, arithmetic and copies ran while one was open for 3% of the time, Pallas kernels for 8%

profile of v2, /device:TPU:2, one launch (start us, length us, event | category | flops | bytes accessed | tf_op | source)
XLA Modules:
  0.0 119.1 jit_solution(14381989710434659288)
XLA Ops:
  0.0 0.0 copy-start
  0.0 0.0 copy-start.1
  0.0 0.8 fusion.2
  0.8 0.8 fusion.3
  1.6 0.7 pad_maximum_fusion
  2.3 4.5 %all-to-all-start.1 = ((bf16[4,64,256]{2,1,0:T(8,128)(2,1)}), bf16[4,64,256]{2,1,0:T(8,128)(2,1)S(1)}, u32[]{:S(2)}, u32[]{:S(2)}) async-start(bf16[4,64,256]{2,1,0:T(8,128)(2,1)} %pad_maximum_fusion), calls=%async_computation.1 | async-start | bytes 262144 | tf_op jit(solution)/shard_map/all_to_all | solution.py:295
  6.8 0.0 copy-done.1
  6.8 0.4 reshape.34
  7.2 0.2 copy.12
  7.3 5.4 %all-to-all-done.1 = bf16[4,64,256]{2,1,0:T(8,128)(2,1)S(1)} async-done(((bf16[4,64,256]{2,1,0:T(8,128)(2,1)}), bf16[4,64,256]{2,1,0:T(8,128)(2,1)S(1)}, u32[]{:S(2)}, u32[]{:S(2)}) %all-to-all-start.1) | async-done | bytes 131104 | tf_op jit(solution)/shard_map/all_to_all | solution.py:295
  12.8 1.1 broadcast_in_dim.13
  13.9 3.8 %all-to-all-start = ((bf16[8,64,1024]{2,1,0:T(8,128)(2,1)}), bf16[8,64,1024]{2,1,0:T(8,128)(2,1)S(1)}, u32[]{:S(2)}, u32[]{:S(2)}) async-start(bf16[8,64,1024]{2,1,0:T(8,128)(2,1)} %bitcast.3), calls=%async_computation | async-start | bytes 2097152 | tf_op jit(solution)/shard_map/all_to_all | solution.py:311
  17.7 0.0 copy-done
  17.7 0.1 reshape.31
  17.8 0.1 reshape.32
  17.9 0.7 dynamic-slice_reduce_fusion.1
  18.7 0.1 copy.11
  18.8 0.1 lt.40
  18.9 0.2 convert_reduce_fusion
  19.1 0.2 convert_reduce_fusion.1
  19.3 37.9 %all-gather = bf16[16,64,256]{2,1,0:T(8,128)(2,1)S(1)} all-gather(bf16[4,64,256]{2,1,0:T(8,128)(2,1)S(1)} %all-to-all-done.1), channel_id=2, replica_groups=mesh['yh'=2,'yl'=2,'za'=4,'zb'=2,'zp'=2,'x'=4,'c'=2] {'za'}, dimensions={0}, use_global_device_ids=true | all-gather | bytes 655360 | tf_op jit(solution)/shard_map/all_gather | solution.py:296
  57.2 5.4 %collective-permute-start.3 = (bf16[2,4,64,256]{3,2,1,0:T(8,128)(2,1)S(1)}, bf16[2,4,64,256]{3,2,1,0:T(8,128)(2,1)S(1)}, u32[]{:S(2)}, u32[]{:S(2)}) collective-permute-start(bf16[2,4,64,256]{3,2,1,0:T(8,128)(2,1)S(1)} %bitcast.23), channel_id=1, source_target_pairs={{0,112},{1,113},{2,114},{3,115},{4,116},{5,117},{6,118},{7,119},{1... | collective-permute-start | bytes 786440 | tf_op jit(solution)/shard_map/ppermute | solution.py:281
  62.6 2.0 %collective-permute-start.4 = (bf16[2,4,64,256]{3,2,1,0:T(8,128)(2,1)S(1)}, bf16[2,4,64,256]{3,2,1,0:T(8,128)(2,1)S(1)}, u32[]{:S(2)}, u32[]{:S(2)}) collective-permute-start(bf16[2,4,64,256]{3,2,1,0:T(8,128)(2,1)S(1)} %bitcast.22), channel_id=1, source_target_pairs={{0,16},{1,17},{2,18},{3,19},{4,20},{5,21},{6,22},{7,23},{16,32},{1... | collective-permute-start | bytes 786440 | tf_op jit(solution)/shard_map/ppermute | solution.py:281
  64.6 0.1 select_reduce_fusion
  64.7 0.1 concatenate.15.info_ref
  64.9 1.9 %collective-permute-start = (bf16[4,2,64,256]{3,2,1,0:T(8,128)(2,1)S(1)}, bf16[4,2,64,256]{3,2,1,0:T(8,128)(2,1)S(1)}, u32[]{:S(2)}, u32[]{:S(2)}) collective-permute-start(bf16[4,2,64,256]{3,2,1,0:T(8,128)(2,1)S(1)} %slice.56), channel_id=1, source_target_pairs={{0,1},{1,2},{2,3},{3,4},{4,5},{5,6},{6,7},{16,17},{17,18},{18,19},... | collective-permute-start | bytes 786440 | tf_op jit(solution)/shard_map/ppermute | solution.py:281
  66.8 0.7 fusion.1
  67.5 7.2 %collective-permute-start.2 = (bf16[2,2,64,256]{3,2,1,0:T(8,128)(2,1)}, bf16[2,2,64,256]{3,2,1,0:T(8,128)(2,1)S(1)}, u32[]{:S(2)}, u32[]{:S(2)}) collective-permute-start(bf16[2,2,64,256]{3,2,1,0:T(8,128)(2,1)} %get-tuple-element.15), channel_id=1, source_target_pairs={{0,17},{1,18},{2,19},{3,20},{4,21},{5,22},{6,23},{16,33},{17,34},{... | collective-permute-start | bytes 393224 | tf_op jit(solution)/shard_map/ppermute | solution.py:281
  74.7 1.9 %collective-permute-start.1 = (bf16[2,2,64,256]{3,2,1,0:T(8,128)(2,1)S(1)}, bf16[2,2,64,256]{3,2,1,0:T(8,128)(2,1)S(1)}, u32[]{:S(2)}, u32[]{:S(2)}) collective-permute-start(bf16[2,2,64,256]{3,2,1,0:T(8,128)(2,1)S(1)} %get-tuple-element.16), channel_id=1, source_target_pairs={{0,113},{1,114},{2,115},{3,116},{4,117},{5,118},{6,119},{16,1},{17... | collective-permute-start | bytes 393224 | tf_op jit(solution)/shard_map/ppermute | solution.py:281
  76.6 0.0 collective-permute-done.3.next_ref
  76.6 0.0 collective-permute-done.4.prev_ref
  76.6 0.0 all-to-all-done.q_ref
  76.6 9.8 %own_part.1 = (f32[8,1,512]{2,1,0:T(1,128)S(1)}, f32[8,1,512]{2,1,0:T(1,128)S(1)}, f32[8,128,512]{2,1,0:T(8,128)S(1)}) custom-call(s32[81]{0:T(128)S(1)} %concatenate.15.info_ref, bf16[8,64,1024]{2,1,0:T(8,128)(2,1)S(1)} %all-to-all-done.q_ref, bf16[4,4,64,256]{3,2,1,0:T(8,128)(2,1)S(1)} %bitcast.20, ...), custom_call_target="tpu_custom_call" | custom-call | flops 2147483648 | bytes 4194304 | tf_op jit(solution)/shard_map/own_part/pallas_call | solution.py:331
  86.5 0.0 collective-permute-done.2.prev_ref
  86.5 0.0 collective-permute-done.1.next_ref
  86.5 0.0 collective-permute-done.far_ref
  86.5 6.7 %earlier_part.1 = bf16[8,64,1152]{2,1,0:T(8,128)(2,1)S(1)} custom-call(s32[81]{0:T(128)S(1)} %concatenate.15.info_ref, bf16[8,64,1024]{2,1,0:T(8,128)(2,1)S(1)} %all-to-all-done.q_ref, bf16[4,2,64,256]{3,2,1,0:T(8,128)(2,1)S(1)} %collective-permute-done.far_ref, bf16[2,2,64,256]{3,2,1,0:T(8,128)(2,1)S(1)} %collective-permute-done.1.next_ref, ...), custom_call_target="tpu_custom_call" | custom-call | flops 2147483648 | bytes 4194304 | tf_op jit(solution)/shard_map/earlier_part/pallas_call | solution.py:349
  93.2 24.3 %all_to_all.15.parts_ref = bf16[8,64,1152]{2,1,0:T(8,128)(2,1)S(1)} all-to-all(bf16[8,64,1152]{2,1,0:T(8,128)(2,1)S(1)} %earlier_part.1), channel_id=1, replica_groups=mesh['yh'=2,'yl'=2,'za'=4,'zb'=2,'zp'=2,'x'=4,'c'=2] {'yh','yl','zp'}, dimensions={0} | all-to-all | bytes 2359296 | tf_op jit(solution)/shard_map/all_to_all | solution.py:362
  117.4 1.7 %join_parts.1 = bf16[64,4096]{1,0:T(8,128)(2,1)} custom-call(bf16[8,64,1152]{2,1,0:T(8,128)(2,1)S(1)} %all_to_all.15.parts_ref), custom_call_target="tpu_custom_call" | custom-call | flops 786432 | bytes 2097152 | tf_op jit(solution)/shard_map/join_parts/pallas_call | solution.py:364
  (7 shorter events, 0.1 us)
Async XLA Ops:
  0.0 17.7 %copy-start = (s32[2,32,8]{1,2,0:T(8,128)S(1)}, s32[2,32,8]{1,2,0:T(8,128)}, u32[]{:S(2)}) copy-start(s32[2,32,8]{1,2,0:T(8,128)} %param.7) | copy-start | bytes 6148
  0.0 6.8 %copy-start.1 = (bf16[64,4096]{1,0:T(8,128)(2,1)S(1)}, bf16[64,4096]{1,0:T(8,128)(2,1)}, u32[]{:S(2)}) copy-start(bf16[64,4096]{1,0:T(8,128)(2,1)} %param.4) | copy-start | bytes 1572868
  2.3 10.4 %all-to-all-start.1 = ((bf16[4,64,256]{2,1,0:T(8,128)(2,1)}), bf16[4,64,256]{2,1,0:T(8,128)(2,1)S(1)}, u32[]{:S(2)}, u32[]{:S(2)}) async-start(bf16[4,64,256]{2,1,0:T(8,128)(2,1)} %pad_maximum_fusion), calls=%async_computation.1 | async-start | bytes 262144 | tf_op jit(solution)/shard_map/all_to_all | solution.py:295
  13.9 62.8 %all-to-all-start = ((bf16[8,64,1024]{2,1,0:T(8,128)(2,1)}), bf16[8,64,1024]{2,1,0:T(8,128)(2,1)S(1)}, u32[]{:S(2)}, u32[]{:S(2)}) async-start(bf16[8,64,1024]{2,1,0:T(8,128)(2,1)} %bitcast.3), calls=%async_computation | async-start | bytes 2097152 | tf_op jit(solution)/shard_map/all_to_all | solution.py:311
  57.2 19.4 %collective-permute-start.3 = (bf16[2,4,64,256]{3,2,1,0:T(8,128)(2,1)S(1)}, bf16[2,4,64,256]{3,2,1,0:T(8,128)(2,1)S(1)}, u32[]{:S(2)}, u32[]{:S(2)}) collective-permute-start(bf16[2,4,64,256]{3,2,1,0:T(8,128)(2,1)S(1)} %bitcast.23), channel_id=1, source_target_pairs={{0,112},{1,113},{2,114},{3,115},{4,116},{5,117},{6,118},{7,119},{1... | collective-permute-start | bytes 786440 | tf_op jit(solution)/shard_map/ppermute | solution.py:281
  62.6 14.1 %collective-permute-start.4 = (bf16[2,4,64,256]{3,2,1,0:T(8,128)(2,1)S(1)}, bf16[2,4,64,256]{3,2,1,0:T(8,128)(2,1)S(1)}, u32[]{:S(2)}, u32[]{:S(2)}) collective-permute-start(bf16[2,4,64,256]{3,2,1,0:T(8,128)(2,1)S(1)} %bitcast.22), channel_id=1, source_target_pairs={{0,16},{1,17},{2,18},{3,19},{4,20},{5,21},{6,22},{7,23},{16,32},{1... | collective-permute-start | bytes 786440 | tf_op jit(solution)/shard_map/ppermute | solution.py:281
  64.9 21.6 %collective-permute-start = (bf16[4,2,64,256]{3,2,1,0:T(8,128)(2,1)S(1)}, bf16[4,2,64,256]{3,2,1,0:T(8,128)(2,1)S(1)}, u32[]{:S(2)}, u32[]{:S(2)}) collective-permute-start(bf16[4,2,64,256]{3,2,1,0:T(8,128)(2,1)S(1)} %slice.56), channel_id=1, source_target_pairs={{0,1},{1,2},{2,3},{3,4},{4,5},{5,6},{6,7},{16,17},{17,18},{18,19},... | collective-permute-start | bytes 786440 | tf_op jit(solution)/shard_map/ppermute | solution.py:281
  67.5 19.0 %collective-permute-start.2 = (bf16[2,2,64,256]{3,2,1,0:T(8,128)(2,1)}, bf16[2,2,64,256]{3,2,1,0:T(8,128)(2,1)S(1)}, u32[]{:S(2)}, u32[]{:S(2)}) collective-permute-start(bf16[2,2,64,256]{3,2,1,0:T(8,128)(2,1)} %get-tuple-element.15), channel_id=1, source_target_pairs={{0,17},{1,18},{2,19},{3,20},{4,21},{5,22},{6,23},{16,33},{17,34},{... | collective-permute-start | bytes 393224 | tf_op jit(solution)/shard_map/ppermute | solution.py:281
  74.7 11.8 %collective-permute-start.1 = (bf16[2,2,64,256]{3,2,1,0:T(8,128)(2,1)S(1)}, bf16[2,2,64,256]{3,2,1,0:T(8,128)(2,1)S(1)}, u32[]{:S(2)}, u32[]{:S(2)}) collective-permute-start(bf16[2,2,64,256]{3,2,1,0:T(8,128)(2,1)S(1)} %get-tuple-element.16), channel_id=1, source_target_pairs={{0,113},{1,114},{2,115},{3,116},{4,117},{5,118},{6,119},{16,1},{17... | collective-permute-start | bytes 393224 | tf_op jit(solution)/shard_map/ppermute | solution.py:281

commit v3 on v2

v3 whole, which is shorter than its diff:
```python
import functools
import math

import jax
import jax.numpy as jnp
from jax import lax
from jax.experimental import pallas as pl
from jax.experimental.pallas import tpu as pltpu
from jax.sharding import Mesh
from jax.sharding import PartitionSpec as P

HD = 128
TOK = 64
KVH = 4
GROUP = 8
ROWS = GROUP * TOK
CHUNK = 256
PER_CHUNK = CHUNK // TOK
LOW = -1e30
SCALE = math.log2(math.e) / math.sqrt(HD)

AXES = ("yh", "yl", "za", "zb", "zp", "x", "c")
LINE = ("yh", "yl")
SHARE = ("yh", "yl", "zp")
DEPTH = ("za", "zb", "zp")
RING = ("za", "zb")
STRETCHES = ("x", "c")
FAR = ((0, 4, 8, 12), (13, 9, 5, 1), (2, 6, 10, 14), (15, 11, 7, 3))
MIB = 1024 * 1024
ONES = 16
SIDE = HD + ONES
PARTS = 1
LEVELS = 16


def stacked_heads(q_ref, b, first=0, count=GROUP):
    return jnp.concatenate(
        [q_ref[b, :, h * HD : (h + 1) * HD] for h in range(first, first + count)], axis=0
    )


def score(keys, query):
    return lax.dot_general(
        keys, query, (((1,), (1,)), ((), ())), preferred_element_type=jnp.float32
    )


def weigh(values_t, scores, top):
    weights = jnp.exp2((scores - top) * SCALE).astype(jnp.bfloat16)
    return jnp.dot(values_t, weights, preferred_element_type=jnp.float32)


def pack_queries_kernel(q_ref, out_ref):
    width = GROUP * HD
    copies = out_ref.shape[0] // KVH
    for m in range(KVH):
        for i in range(copies):
            out_ref[m * copies + i] = q_ref[:, m * width : (m + 1) * width]


def own_kernel(first, info_ref, q_ref, lower_ref, upper_ref, *refs):
    if not first:
        state_in, refs = refs[:3], refs[3:]
    top_ref, total_ref, sum_ref, k_s, v_s, vt_s, lead_s, score_s, top_s, piece_s, piece_top = refs
    half = lower_ref.shape[0] * 2
    for i in range(2 * half):
        place, line = i % half // 2, i % 2
        block = (lower_ref if i < half else upper_ref)[place, line]
        at = pl.ds(pl.multiple_of(info_ref[i] * TOK, TOK), TOK)
        k_s[at, :] = block[:, :HD]
        v_s[at, :] = block[:, HD:]
    count = k_s.shape[0]
    for j in range(0, count, CHUNK):
        vt_s[:HD, j : j + CHUNK] = v_s[j : j + CHUNK, :].T
    vt_s[HD:, :] = jnp.ones((ONES, count), jnp.bfloat16)
    key_row = lax.broadcasted_iota(jnp.int32, (TOK, ROWS), 0)
    query_row = lax.broadcasted_iota(jnp.int32, (TOK, ROWS), 1) % TOK
    lead_s[...] = query_row - key_row
    blocks = q_ref.shape[0]
    pairs = blocks // 2
    lower = count // 2
    numbers, queries, seen = 2 * half, 4 * half, 4 * half + blocks
    if first:
        top_ref[...] = jnp.full(top_ref.shape, LOW, jnp.float32)
        total_ref[...] = jnp.zeros(total_ref.shape, jnp.float32)
        sum_ref[...] = jnp.zeros(sum_ref.shape, jnp.float32)
    else:
        for ref, ref_in in zip((top_ref, total_ref, sum_ref), state_in):
            ref[...] = ref_in[...]

    def add(b, values_t, scores, top_new):
        old = top_ref[b]
        top = jnp.maximum(old, top_new)
        both = weigh(values_t, scores, top)
        factor = jnp.exp2((old - top) * SCALE)
        top_ref[b] = top
        total_ref[b] = total_ref[b] * factor + both[HD : HD + 1]
        sum_ref[b] = sum_ref[b] * factor + both[:HD]

    def begin(b, slot):
        scores = score(k_s[:lower, :], stacked_heads(q_ref, b))
        score_s[slot] = scores
        top_s[slot] = jnp.max(scores, axis=0, keepdims=True)

    def end(b, slot):
        add(b, vt_s[:, :lower], score_s[slot], top_s[slot])

    steps = lower // CHUNK + 1
    items = pairs * steps

    def place_of(item):
        pair, step = item // steps, item % steps
        low = (info_ref[seen + pair] + PER_CHUNK - 1) // PER_CHUNK
        high = (info_ref[seen + pairs + pair] - half + PER_CHUNK - 1) // PER_CHUNK
        is_low = step < low
        b = jnp.where(is_low, pair, pairs + pair)
        chunk = jnp.where(is_low, step, jnp.minimum(steps - 1 + step - low, 2 * steps - 3))
        own = jnp.where(step < low + high, info_ref[queries + b], -4096)
        return b, chunk, own

    def begin_item(item, slot):
        b, chunk, own = place_of(item)
        at = pl.ds(pl.multiple_of(chunk * CHUNK, CHUNK), CHUNK)
        scores = score(k_s[at, :], stacked_heads(q_ref, b))
        top = None
        for i in range(PER_CHUNK):
            ahead = (info_ref[numbers + chunk * PER_CHUNK + i] - own) * TOK
            part = scores[i * TOK : (i + 1) * TOK]
            part = jnp.where(lead_s[...] >= ahead, part, LOW)
            piece_s[slot, i * TOK : (i + 1) * TOK, :] = part
            high = jnp.max(part, axis=0, keepdims=True)
            top = high if top is None else jnp.maximum(top, high)
        piece_top[slot] = top

    def end_item(item, slot):
        b, chunk, own = place_of(item)
        at = pl.ds(pl.multiple_of(chunk * CHUNK, CHUNK), CHUNK)
        add(b, vt_s[:, at], piece_s[slot], piece_top[slot])

    begin(pairs, 0)
    begin(pairs + 1, 1)
    begin(pairs + 2, 2)
    end(pairs, 0)
    begin(pairs + 3, 3)
    end(pairs + 1, 1)
    begin_item(0, 0)
    end(pairs + 2, 2)
    begin_item(1, 1)
    end(pairs + 3, 3)

    @pl.loop(0, items // 4)
    def _(i):
        begin_item(4 * i + 2, 2)
        begin_item(4 * i + 3, 3)
        end_item(4 * i, 0)
        end_item(4 * i + 1, 1)
        begin_item(jnp.minimum(4 * i + 4, items - 1), 0)
        begin_item(jnp.minimum(4 * i + 5, items - 1), 1)
        end_item(4 * i + 2, 2)
        end_item(4 * i + 3, 3)


def earlier_kernel(
    part, info_ref, q_ref, far_ref, prev_ref, top_in, total_in, sum_in, out_ref,
    k_s, vt_s, score_s, top_s,
):
    cols = score_s.shape[2]
    heads = cols // TOK
    here = slice(part * cols, (part + 1) * cols)

    def finish(b, top, total, summed):
        some = total > 0.0
        safe = jnp.where(some, total, 1.0)
        out_ref[b, :cols, :] = (summed * (1.0 / safe)).T.astype(jnp.bfloat16)
        level = jnp.where(some, top * SCALE + jnp.log2(safe), LOW)
        level = jnp.concatenate([level[:, j : j + HD] for j in range(0, cols, HD)], axis=0)
        high = level.astype(jnp.bfloat16).astype(jnp.float32)
        middle = (level - high).astype(jnp.bfloat16).astype(jnp.float32)
        unused = jnp.zeros((LEVELS - 3 * (cols // HD), HD), jnp.float32)
        pieces = jnp.concatenate([high, middle, level - high - middle, unused], axis=0)
        out_ref[b, cols:, :] = pieces.astype(jnp.bfloat16)

    blocks = q_ref.shape[0]

    @pl.when(info_ref[0] == 0)
    def _():
        @pl.loop(0, blocks)
        def _(b):
            finish(b, top_in[b, :, here], total_in[b, :, here], sum_in[b, :, here])

    @pl.when(info_ref[0] > 0)
    def _():
        at = 0
        for ref in (far_ref, prev_ref):
            rows = ref.shape[0] * ref.shape[1] * TOK
            flat = ref[...].reshape(rows, 2 * HD)
            k_s[at : at + rows, :] = flat[:, :HD]
            for j in range(0, rows, CHUNK):
                vt_s[:HD, at + j : at + j + CHUNK] = flat[j : j + CHUNK, HD:].T
            at += rows
        vt_s[HD:, :] = jnp.ones((ONES, at), jnp.bfloat16)

        def begin(b, slot):
            scores = score(k_s[...], stacked_heads(q_ref, b, part * heads, heads))
            score_s[slot] = scores
            top_s[slot] = jnp.max(scores, axis=0, keepdims=True)

        def end(b, slot):
            old = top_in[b, :, here]
            top = jnp.maximum(old, top_s[slot])
            both = weigh(vt_s[...], score_s[slot], top)
            factor = jnp.exp2((old - top) * SCALE)
            finish(
                b,
                top,
                total_in[b, :, here] * factor + both[HD : HD + 1],
                sum_in[b, :, here] * factor + both[:HD],
            )

        begin(0, 0)

        @pl.loop(0, blocks // 2)
        def _(i):
            begin(2 * i + 1, 1)
            end(2 * i, 0)
            begin(jnp.minimum(2 * i + 2, blocks - 1), 0)
            end(2 * i + 1, 1)


def join_kernel(*refs):
    parts_refs, out_ref = refs[:-1], refs[-1]
    cols = parts_refs[0].shape[1] - LEVELS
    rows, heads = cols // HD, cols // TOK
    for part, parts_ref in enumerate(parts_refs):
        for m in range(KVH):
            level = []
            for p in range(2):
                pieces = parts_ref[2 * m + p, cols:, :].astype(jnp.float32)
                level.append(
                    pieces[:rows] + pieces[rows : 2 * rows] + pieces[2 * rows : 3 * rows]
                )
            share = 1.0 / (1.0 + jnp.exp2(level[1] - level[0]))
            share = jnp.concatenate([share, jnp.zeros((8 - rows, HD), jnp.float32)], axis=0).T
            for h in range(heads):
                at = h * TOK
                first = parts_ref[2 * m, at : at + TOK, :].astype(jnp.float32)
                second = parts_ref[2 * m + 1, at : at + TOK, :].astype(jnp.float32)
                mine = share[at % HD : at % HD + TOK, at // HD : at // HD + 1]
                mixed = second + (first - second) * mine
                at = (m * GROUP + part * heads + h) * HD
                out_ref[:, at : at + HD] = mixed.astype(jnp.bfloat16)


def in_vmem():
    return pl.BlockSpec(memory_space=pltpu.VMEM)


def in_smem():
    return pl.BlockSpec(memory_space=pltpu.SMEM)


def tables(block_order):
    za, zb, zp = (lax.axis_index(name) for name in ("za", "zb", "zp"))
    stretch = lax.axis_index(STRETCHES)
    ids = lax.dynamic_index_in_dim(block_order, stretch, 2, keepdims=False)
    ids = ids.reshape(2, 2, lax.axis_size("za"), lax.axis_size("zb"), lax.axis_size("zp"))
    keys = lax.dynamic_index_in_dim(ids, zp, 4, keepdims=False)
    keys = jnp.where(zp == 1, keys[:, :, ::-1], keys)
    near = lax.dynamic_index_in_dim(keys, zb, 3, keepdims=False)
    other = lax.dynamic_index_in_dim(keys, 1 - zb, 3, keepdims=False)
    keys = jnp.stack([near, other]).transpose(0, 1, 3, 2).reshape(2, -1)
    queries = lax.dynamic_index_in_dim(ids, za, 2, keepdims=False)
    queries = lax.dynamic_index_in_dim(queries, zb, 2, keepdims=False).reshape(-1)
    place = jnp.sum(keys[:, None, :] < keys[:, :, None], axis=2, dtype=jnp.int32)
    slots = jnp.arange(keys.shape[1], dtype=jnp.int32)
    there = place[:, None, :] == slots[None, :, None]
    in_order = jnp.sum(jnp.where(there, keys[:, None, :], 0), axis=2)
    seen = jnp.sum(keys[:, None, :] <= queries[None, :, None], axis=2, dtype=jnp.int32)
    queries = jnp.broadcast_to(queries, seen.shape)
    table = jnp.concatenate([place, in_order, queries, seen], axis=1)
    return table[0], table[1], stretch.reshape(1)


def along(block, axis, step, around):
    count = lax.axis_size(axis)
    route = [(i, (i + step) % count) for i in range(count) if around or i + step < count]
    return lax.ppermute(block, axis, route)


def body(queries, keys, values, block_order):
    tokens = queries.shape[0]
    lines = KVH
    params = pltpu.CompilerParams(vmem_limit_bytes=40 * MIB)
    pairs = lax.axis_size("zp")
    width = GROUP * HD
    kv = jnp.stack(
        [
            jnp.concatenate(
                [keys[:, m * HD : (m + 1) * HD], values[:, m * HD : (m + 1) * HD]], axis=1
            )
            for m in range(lines)
        ]
    )
    own = lax.all_to_all(kv, LINE, split_axis=0, concat_axis=0, tiled=True)
    info_near, info_other, stretch = tables(block_order)

    with jax.named_scope("pack_queries"):
        split = pl.pallas_call(
            pack_queries_kernel,
            out_shape=jax.ShapeDtypeStruct((lines * pairs, tokens, width), jnp.bfloat16),
            in_specs=[in_vmem()],
            out_specs=in_vmem(),
            compiler_params=params,
            cost_estimate=pl.CostEstimate(flops=0, bytes_accessed=2 * MIB, transcendentals=0),
        )(queries)
    own, split, info_near, info_other, stretch = lax.optimization_barrier(
        (own, split, info_near, info_other, stretch)
    )
    far = lax.all_gather(own, DEPTH, axis=0, axis_index_groups=FAR)
    lower, upper = far[:, :2], far[:, 2:]
    own_next = along(lower, RING, -1, True)
    own_prev = along(upper, RING, 1, True)
    earlier_far = along(upper, STRETCHES, 1, False)
    earlier_prev = along(own_prev, STRETCHES, 1, False)
    query = lax.all_to_all(split, SHARE, split_axis=0, concat_axis=0, tiled=True)
    blocks = lines * pairs

    count = lax.axis_size(RING) * 2 * TOK
    state = [
        jax.ShapeDtypeStruct((blocks, 1, ROWS), jnp.float32),
        jax.ShapeDtypeStruct((blocks, 1, ROWS), jnp.float32),
        jax.ShapeDtypeStruct((blocks, HD, ROWS), jnp.float32),
    ]
    cost = pl.CostEstimate(
        flops=4 * blocks * ROWS * count * HD,
        bytes_accessed=4 * MIB,
        transcendentals=blocks * ROWS * count,
    )
    half = count // 2

    def own_part(first, info, lower, upper, *state_in):
        return pl.pallas_call(
            functools.partial(own_kernel, first),
            out_shape=state,
            in_specs=[in_smem()] + [in_vmem()] * (3 + len(state_in)),
            out_specs=[in_vmem()] * 3,
            scratch_shapes=[
                pltpu.VMEM((count, HD), jnp.bfloat16),
                pltpu.VMEM((count, HD), jnp.bfloat16),
                pltpu.VMEM((SIDE, count), jnp.bfloat16),
                pltpu.VMEM((TOK, ROWS), jnp.int32),
                pltpu.VMEM((4, half, ROWS), jnp.float32),
                pltpu.VMEM((4, 1, ROWS), jnp.float32),
                pltpu.VMEM((4, CHUNK, ROWS), jnp.float32),
                pltpu.VMEM((4, 1, ROWS), jnp.float32),
            ],
            compiler_params=params,
            cost_estimate=cost,
        )(info, query, lower, upper, *state_in)

    with jax.named_scope("own_near"):
        sums = own_part(True, info_near, lower, upper)
    with jax.named_scope("own_other"):
        sums = own_part(False, info_other, own_next, own_prev, *sums)
    cols = ROWS // PARTS
    joined = []
    for i in range(PARTS):
        with jax.named_scope("earlier_part"):
            part = pl.pallas_call(
                functools.partial(earlier_kernel, i),
                out_shape=jax.ShapeDtypeStruct((blocks, cols + LEVELS, HD), jnp.bfloat16),
                in_specs=[in_smem()] + [in_vmem()] * 6,
                out_specs=in_vmem(),
                scratch_shapes=[
                    pltpu.VMEM((count, HD), jnp.bfloat16),
                    pltpu.VMEM((SIDE, count), jnp.bfloat16),
                    pltpu.VMEM((2, count, cols), jnp.float32),
                    pltpu.VMEM((2, 1, cols), jnp.float32),
                ],
                compiler_params=params,
                cost_estimate=cost,
            )(stretch, query, earlier_far, earlier_prev, *sums)
        joined.append(lax.all_to_all(part, SHARE, split_axis=0, concat_axis=0, tiled=True))
    with jax.named_scope("join_parts"):
        return pl.pallas_call(
            join_kernel,
            out_shape=jax.ShapeDtypeStruct((tokens, lines * width), jnp.bfloat16),
            in_specs=[in_vmem()] * PARTS,
            out_specs=in_vmem(),
            compiler_params=params,
            cost_estimate=pl.CostEstimate(
                flops=3 * tokens * lines * width, bytes_accessed=2 * MIB, transcendentals=0
            ),
        )(*joined)


def solution(mesh):
    fine = Mesh(mesh.devices.reshape(2, 2, 4, 2, 2, 4, 2), AXES)
    rows = P(AXES, None)
    return jax.shard_map(
        body, mesh=fine, in_specs=(rows, rows, rows, P()), out_specs=rows, check_vma=False
    )
```

time: 120 us -> 112 us (0.933)
  starting transfers between devices: 26.8 us -> 21.7 us
  waiting for transfers between devices: 5.45 us -> 3.61 us
  local copies, waits for them, and re-layouts: 5.27 us -> 3.49 us
    ppermute x5 -> x4, starting transfers between devices: 18.5 us -> 13.4 us  [along(): return lax.ppermute(block, axis, route)]
    all_to_all x1, waiting for transfers between devices: 5.43 us -> 2.44 us  [body(): own = lax.all_to_all(kv, LINE, split_axis=0, concat_axis=0, tiled=True)]
    pallas_call x2 -> x4, Pallas kernels: 16.5 us -> 16.9 us  [the longest x2 10.2 us: own_part(): pl.pallas_call(functools.partial(own_kernel, first), out_shape=state, in_...]
  transfers between devices with their start and end apart: 7 -> 6, of which waited for: 1 -> 2; matrix products, arithmetic and copies ran while one was open for 3% -> 1% of each run, Pallas kernels for 8% -> 10%
where the time goes in v3:
time: 112 us; the launch traced here: 111 us
  blocking collectives  63 us (56%)
  starting transfers between devices  21.7 us (19%)
  Pallas kernels  18.3 us (16%)
  waiting for transfers between devices  3.61 us (3%)
  local copies, waits for them, and re-layouts  3.49 us (3%)
  other arithmetic  1.27 us (1%)
    all_gather x1, blocking collectives, body(): far = lax.all_gather(own, DEPTH, axis=0, axis_index_groups=FAR)  38.1 us
    all_to_all x1, blocking collectives, body(): lax.all_to_all(part, SHARE, split_axis=0, concat_axis=0, tiled=True)  24.9 us
    ppermute x4, starting transfers between devices, along(): return lax.ppermute(block, axis, route)  13.4 us
    pallas_call x2, Pallas kernels, own_part(): pl.pallas_call(functools.partial(own_kernel, first), out_shape=state, in_...  10.2 us
    pallas_call x1, Pallas kernels, body(): pl.pallas_call(functools.partial(earlier_kernel, i), out_shape=jax.ShapeD...  5.72 us
    all_to_all x1, starting transfers between devices, body(): own = lax.all_to_all(kv, LINE, split_axis=0, concat_axis=0, tiled=True)  4.46 us
    all_to_all x1, starting transfers between devices, body(): lax.all_to_all(split, SHARE, split_axis=0, concat_axis=0, tiled=True)  3.8 us
    all_to_all x1, waiting for transfers between devices, body(): own = lax.all_to_all(kv, LINE, split_axis=0, concat_axis=0, tiled=True)  2.44 us
  transfers between devices with their start and end apart: 6, of which 2 were waited for; matrix products, arithmetic and copies ran while one was open for 1% of the time, Pallas kernels for 10%

profile of v3, /device:TPU:2, one launch (start us, length us, event | category | flops | bytes accessed | tf_op | source)
XLA Modules:
  0.0 111.5 jit_solution(3859101345143772436)
XLA Ops:
  0.0 0.0 copy-start
  0.0 0.8 fusion.2
  0.8 0.8 fusion.3
  1.6 0.7 pad_maximum_fusion
  2.3 4.5 %all-to-all-start = ((bf16[4,64,256]{2,1,0:T(8,128)(2,1)}), bf16[4,64,256]{2,1,0:T(8,128)(2,1)S(1)}, u32[]{:S(2)}, u32[]{:S(2)}) async-start(bf16[4,64,256]{2,1,0:T(8,128)(2,1)} %pad_maximum_fusion), calls=%async_computation | async-start | bytes 262144 | tf_op jit(solution)/shard_map/all_to_all | solution.py:304
  6.7 0.0 copy-done
  6.8 0.1 reshape.20
  6.9 0.1 constant_dynamic-slice_fusion.2
  6.9 0.1 copy.11
  7.1 0.1 rev.3
  7.2 0.1 copy.12
  7.3 0.1 lt.40
  7.4 0.2 convert_reduce_fusion
  7.6 0.1 reshape.35
  7.7 0.2 convert_reduce_fusion.1
  7.9 0.1 pad.2.clone
  8.0 0.1 select_reduce_fusion
  8.1 0.1 pad_add_fusion
  8.2 0.0 copy-start.1
  8.2 1.0 copy-done.1
  9.2 1.0 pack_queries.1
  10.3 2.4 %all-to-all-done = bf16[4,64,256]{2,1,0:T(8,128)(2,1)S(1)} async-done(((bf16[4,64,256]{2,1,0:T(8,128)(2,1)}), bf16[4,64,256]{2,1,0:T(8,128)(2,1)S(1)}, u32[]{:S(2)}, u32[]{:S(2)}) %all-to-all-start) | async-done | bytes 131104 | tf_op jit(solution)/shard_map/all_to_all | solution.py:304
  12.7 3.8 %all-to-all-start.1 = ((bf16[8,64,1024]{2,1,0:T(8,128)(2,1)}), bf16[8,64,1024]{2,1,0:T(8,128)(2,1)S(1)}, u32[]{:S(2)}, u32[]{:S(2)}) async-start(bf16[8,64,1024]{2,1,0:T(8,128)(2,1)} %pack_queries.1), calls=%async_computation.1 | async-start | bytes 2097152 | tf_op jit(solution)/shard_map/all_to_all | solution.py:325
  16.5 38.1 %all-gather = bf16[16,64,256]{2,1,0:T(8,128)(2,1)S(1)} all-gather(bf16[4,64,256]{2,1,0:T(8,128)(2,1)S(1)} %all-to-all-done), channel_id=2, replica_groups={{0,32,64,96},{104,72,40,8},{16,48,80,112},{120,88,56,24},{1,33,65,97},{..., dimensions={0}, use_global_device_ids=true | all-gather | bytes 655360 | tf_op jit(solution)/shard_map/all_gather | solution.py:319
  54.7 7.1 %collective-permute-start.1 = (bf16[4,2,64,256]{3,2,1,0:T(8,128)(2,1)S(1)}, bf16[4,2,64,256]{3,2,1,0:T(8,128)(2,1)S(1)}, u32[]{:S(2)}, u32[]{:S(2)}) collective-permute-start(bf16[4,2,64,256]{3,2,1,0:T(8,128)(2,1)S(1)} %get-tuple-element.28.upper_ref), channel_id=1, source_target_pairs={{0,16},{16,32},{32,48},{48,64},{64,80},{80,96},{96,112},{112,0},{1... | collective-permute-start | bytes 786440 | tf_op jit(solution)/shard_map/ppermute | solution.py:287
  61.8 2.1 %collective-permute-start.3 = (bf16[4,2,64,256]{3,2,1,0:T(8,128)(2,1)S(1)}, bf16[4,2,64,256]{3,2,1,0:T(8,128)(2,1)S(1)}, u32[]{:S(2)}, u32[]{:S(2)}) collective-permute-start(bf16[4,2,64,256]{3,2,1,0:T(8,128)(2,1)S(1)} %get-tuple-element.27.lower_ref), channel_id=1, source_target_pairs={{0,112},{16,0},{32,16},{48,32},{64,48},{80,64},{96,80},{112,96},{1... | collective-permute-start | bytes 786440 | tf_op jit(solution)/shard_map/ppermute | solution.py:287
  63.8 1.9 %collective-permute-start = (bf16[4,2,64,256]{3,2,1,0:T(8,128)(2,1)S(1)}, bf16[4,2,64,256]{3,2,1,0:T(8,128)(2,1)S(1)}, u32[]{:S(2)}, u32[]{:S(2)}) collective-permute-start(bf16[4,2,64,256]{3,2,1,0:T(8,128)(2,1)S(1)} %get-tuple-element.28.upper_ref), channel_id=1, source_target_pairs={{0,1},{1,2},{2,3},{3,4},{4,5},{5,6},{6,7},{8,9},{9,10},{10,11},{11... | collective-permute-start | bytes 786440 | tf_op jit(solution)/shard_map/ppermute | solution.py:287
  65.7 1.2 %collective-permute-done.1.upper_ref = bf16[4,2,64,256]{3,2,1,0:T(8,128)(2,1)S(1)} collective-permute-done((bf16[4,2,64,256]{3,2,1,0:T(8,128)(2,1)S(1)}, bf16[4,2,64,256]{3,2,1,0:T(8,128)(2,1)S(1)}, u32[]{:S(2)}, u32[]{:S(2)}) %collective-permute-start.1) | collective-permute-done | bytes 262176 | tf_op jit(solution)/shard_map/ppermute | solution.py:287
  66.9 2.4 %collective-permute-start.2 = (bf16[4,2,64,256]{3,2,1,0:T(8,128)(2,1)S(1)}, bf16[4,2,64,256]{3,2,1,0:T(8,128)(2,1)S(1)}, u32[]{:S(2)}, u32[]{:S(2)}) collective-permute-start(bf16[4,2,64,256]{3,2,1,0:T(8,128)(2,1)S(1)} %collective-permute-done.1.upper_ref), channel_id=1, source_target_pairs={{0,1},{1,2},{2,3},{3,4},{4,5},{5,6},{6,7},{8,9},{9,10},{10,11},{11... | collective-permute-start | bytes 786440 | tf_op jit(solution)/shard_map/ppermute | solution.py:287
  69.3 0.0 all-to-all-done.1.q_ref
  69.3 5.1 %own_near.1 = (f32[8,1,512]{2,1,0:T(1,128)S(1)}, f32[8,1,512]{2,1,0:T(1,128)S(1)}, f32[8,128,512]{2,1,0:T(8,128)S(1)}) custom-call(s32[48]{0:T(128)S(1)} %get-tuple-element.20.info_ref, bf16[8,64,1024]{2,1,0:T(8,128)(2,1)S(1)} %all-to-all-done.1.q_ref, bf16[4,2,64,256]{3,2,1,0:T(8,128)(2,1)S(1)} %get-tuple-element.27.lower_ref, ...), custom_call_target="tpu_custom_call" | custom-call | flops 2147483648 | bytes 4194304 | tf_op jit(solution)/shard_map/own_near/pallas_call | solution.py:342
  74.4 0.0 collective-permute-done.3.lower_ref
  74.4 5.1 %own_other.1 = (f32[8,1,512]{2,1,0:T(1,128)S(1)}, f32[8,1,512]{2,1,0:T(1,128)S(1)}, f32[8,128,512]{2,1,0:T(8,128)S(1)}) custom-call(s32[48]{0:T(128)S(1)} %get-tuple-element.19.info_ref, bf16[8,64,1024]{2,1,0:T(8,128)(2,1)S(1)} %all-to-all-done.1.q_ref, bf16[4,2,64,256]{3,2,1,0:T(8,128)(2,1)S(1)} %collective-permute-done.3.lower_ref, ...), custom_call_target="tpu_custom_call" | custom-call | flops 2147483648 | bytes 4194304 | tf_op jit(solution)/shard_map/own_other/pallas_call | solution.py:342
  79.5 0.0 collective-permute-done.far_ref
  79.5 0.0 collective-permute-done.2.prev_ref
  79.5 5.7 %earlier_part.1 = bf16[8,528,128]{2,1,0:T(8,128)(2,1)S(1)} custom-call(s32[1]{0:T(128)} %bitcast.10.info_ref, bf16[8,64,1024]{2,1,0:T(8,128)(2,1)S(1)} %all-to-all-done.1.q_ref, bf16[4,2,64,256]{3,2,1,0:T(8,128)(2,1)S(1)} %collective-permute-done.far_ref, bf16[4,2,64,256]{3,2,1,0:T(8,128)(2,1)S(1)} %collective-permute-done.2.prev_ref, ...), custom_call_target="tpu_custom_call" | custom-call | flops 2147483648 | bytes 4194304 | tf_op jit(solution)/shard_map/earlier_part/pallas_call | solution.py:369
  85.2 24.9 %all_to_all.15.refs_0_ = bf16[8,528,128]{2,1,0:T(8,128)(2,1)S(1)} all-to-all(bf16[8,528,128]{2,1,0:T(8,128)(2,1)S(1)} %earlier_part.1), channel_id=1, replica_groups=mesh['yh'=2,'yl'=2,'za'=4,'zb'=2,'zp'=2,'x'=4,'c'=2] {'yh','yl','zp'}, dimensions={0} | all-to-all | bytes 2162688 | tf_op jit(solution)/shard_map/all_to_all | solution.py:383
  110.2 1.3 %join_parts.1 = bf16[64,4096]{1,0:T(8,128)(2,1)} custom-call(bf16[8,528,128]{2,1,0:T(8,128)(2,1)S(1)} %all_to_all.15.refs_0_), custom_call_target="tpu_custom_call" | custom-call | flops 786432 | bytes 2097152 | tf_op jit(solution)/shard_map/join_parts/pallas_call | solution.py:385
  (9 shorter events, 0.1 us)
Async XLA Ops:
  0.0 6.7 %copy-start = (s32[2,32,8]{1,2,0:T(8,128)S(1)}, s32[2,32,8]{1,2,0:T(8,128)}, u32[]{:S(2)}) copy-start(s32[2,32,8]{1,2,0:T(8,128)} %param.7) | copy-start | bytes 6148
  2.3 10.4 %all-to-all-start = ((bf16[4,64,256]{2,1,0:T(8,128)(2,1)}), bf16[4,64,256]{2,1,0:T(8,128)(2,1)S(1)}, u32[]{:S(2)}, u32[]{:S(2)}) async-start(bf16[4,64,256]{2,1,0:T(8,128)(2,1)} %pad_maximum_fusion), calls=%async_computation | async-start | bytes 262144 | tf_op jit(solution)/shard_map/all_to_all | solution.py:304
  8.2 1.1 copy-start.1
  12.7 56.6 %all-to-all-start.1 = ((bf16[8,64,1024]{2,1,0:T(8,128)(2,1)}), bf16[8,64,1024]{2,1,0:T(8,128)(2,1)S(1)}, u32[]{:S(2)}, u32[]{:S(2)}) async-start(bf16[8,64,1024]{2,1,0:T(8,128)(2,1)} %pack_queries.1), calls=%async_computation.1 | async-start | bytes 2097152 | tf_op jit(solution)/shard_map/all_to_all | solution.py:325
  54.7 12.2 %collective-permute-start.1 = (bf16[4,2,64,256]{3,2,1,0:T(8,128)(2,1)S(1)}, bf16[4,2,64,256]{3,2,1,0:T(8,128)(2,1)S(1)}, u32[]{:S(2)}, u32[]{:S(2)}) collective-permute-start(bf16[4,2,64,256]{3,2,1,0:T(8,128)(2,1)S(1)} %get-tuple-element.28.upper_ref), channel_id=1, source_target_pairs={{0,16},{16,32},{32,48},{48,64},{64,80},{80,96},{96,112},{112,0},{1... | collective-permute-start | bytes 786440 | tf_op jit(solution)/shard_map/ppermute | solution.py:287
  61.8 12.6 %collective-permute-start.3 = (bf16[4,2,64,256]{3,2,1,0:T(8,128)(2,1)S(1)}, bf16[4,2,64,256]{3,2,1,0:T(8,128)(2,1)S(1)}, u32[]{:S(2)}, u32[]{:S(2)}) collective-permute-start(bf16[4,2,64,256]{3,2,1,0:T(8,128)(2,1)S(1)} %get-tuple-element.27.lower_ref), channel_id=1, source_target_pairs={{0,112},{16,0},{32,16},{48,32},{64,48},{80,64},{96,80},{112,96},{1... | collective-permute-start | bytes 786440 | tf_op jit(solution)/shard_map/ppermute | solution.py:287
  63.8 15.7 %collective-permute-start = (bf16[4,2,64,256]{3,2,1,0:T(8,128)(2,1)S(1)}, bf16[4,2,64,256]{3,2,1,0:T(8,128)(2,1)S(1)}, u32[]{:S(2)}, u32[]{:S(2)}) collective-permute-start(bf16[4,2,64,256]{3,2,1,0:T(8,128)(2,1)S(1)} %get-tuple-element.28.upper_ref), channel_id=1, source_target_pairs={{0,1},{1,2},{2,3},{3,4},{4,5},{5,6},{6,7},{8,9},{9,10},{10,11},{11... | collective-permute-start | bytes 786440 | tf_op jit(solution)/shard_map/ppermute | solution.py:287
  66.9 12.6 %collective-permute-start.2 = (bf16[4,2,64,256]{3,2,1,0:T(8,128)(2,1)S(1)}, bf16[4,2,64,256]{3,2,1,0:T(8,128)(2,1)S(1)}, u32[]{:S(2)}, u32[]{:S(2)}) collective-permute-start(bf16[4,2,64,256]{3,2,1,0:T(8,128)(2,1)S(1)} %collective-permute-done.1.upper_ref), channel_id=1, source_target_pairs={{0,1},{1,2},{2,3},{3,4},{4,5},{5,6},{6,7},{8,9},{9,10},{10,11},{11... | collective-permute-start | bytes 786440 | tf_op jit(solution)/shard_map/ppermute | solution.py:287

commit v4 on v3

--- a/solution.py
+++ b/solution.py
@@ -58,9 +58,19 @@
             out_ref[m * copies + i] = q_ref[:, m * width : (m + 1) * width]
 
 
-def own_kernel(first, info_ref, q_ref, lower_ref, upper_ref, *refs):
+def own_kernel(first, core, info_ref, *refs):
+    if core is None:
+        attend_own(first, info_ref, *refs)
+    else:
+
+        @pl.when(lax.rem(info_ref[info_ref.shape[0] - 1], 2) == core)
+        def _():
+            attend_own(first, info_ref, *refs)
+
+
+def attend_own(first, info_ref, q_ref, lower_ref, upper_ref, *refs):
     if not first:
-        state_in, refs = refs[:3], refs[3:]
+        state_0, state_1, refs = refs[:3], refs[3:6], refs[6:]
     top_ref, total_ref, sum_ref, k_s, v_s, vt_s, lead_s, score_s, top_s, piece_s, piece_top = refs
     half = lower_ref.shape[0] * 2
     for i in range(2 * half):
@@ -85,8 +95,13 @@
         total_ref[...] = jnp.zeros(total_ref.shape, jnp.float32)
         sum_ref[...] = jnp.zeros(sum_ref.shape, jnp.float32)
     else:
-        for ref, ref_in in zip((top_ref, total_ref, sum_ref), state_in):
-            ref[...] = ref_in[...]
+        core = lax.rem(info_ref[info_ref.shape[0] - 1], 2)
+        for at, state_in in enumerate((state_0, state_1)):
+
+            @pl.when(core == at)
+            def _(state_in=state_in):
+                for ref, ref_in in zip((top_ref, total_ref, sum_ref), state_in):
+                    ref[...] = ref_in[...]
 
     def add(b, values_t, scores, top_new):
         old = top_ref[b]
@@ -277,7 +292,8 @@
     in_order = jnp.sum(jnp.where(there, keys[:, None, :], 0), axis=2)
     seen = jnp.sum(keys[:, None, :] <= queries[None, :, None], axis=2, dtype=jnp.int32)
     queries = jnp.broadcast_to(queries, seen.shape)
-    table = jnp.concatenate([place, in_order, queries, seen], axis=1)
+    stretches = jnp.broadcast_to(stretch, (2, 1))
+    table = jnp.concatenate([place, in_order, queries, seen, stretches], axis=1)
     return table[0], table[1], stretch.reshape(1)
 
 
@@ -320,8 +336,6 @@
     lower, upper = far[:, :2], far[:, 2:]
     own_next = along(lower, RING, -1, True)
     own_prev = along(upper, RING, 1, True)
-    earlier_far = along(upper, STRETCHES, 1, False)
-    earlier_prev = along(own_prev, STRETCHES, 1, False)
     query = lax.all_to_all(split, SHARE, split_axis=0, concat_axis=0, tiled=True)
     blocks = lines * pairs
 
@@ -338,9 +352,9 @@
     )
     half = count // 2
 
-    def own_part(first, info, lower, upper, *state_in):
+    def own_part(core, info, lower, upper, *state_in):
         return pl.pallas_call(
-            functools.partial(own_kernel, first),
+            functools.partial(own_kernel, not state_in, core),
             out_shape=state,
             in_specs=[in_smem()] + [in_vmem()] * (3 + len(state_in)),
             out_specs=[in_vmem()] * 3,
@@ -358,10 +372,17 @@
             cost_estimate=cost,
         )(info, query, lower, upper, *state_in)
 
-    with jax.named_scope("own_near"):
-        sums = own_part(True, info_near, lower, upper)
+    with jax.named_scope("own_near_core_1"):
+        sums_1 = own_part(1, info_near, lower, upper)
+    onward, *sums_1 = lax.optimization_barrier((upper, *sums_1))
+    own_prev, sums_1[0] = lax.optimization_barrier((own_prev, sums_1[0]))
+    earlier_prev = along(own_prev, STRETCHES, 1, False)
+    earlier_far = along(onward, STRETCHES, 1, False)
+    own_prev, lower, upper = lax.optimization_barrier((own_prev, lower, upper))
+    with jax.named_scope("own_near_core_0"):
+        sums_0 = own_part(0, info_near, lower, upper)
     with jax.named_scope("own_other"):
-        sums = own_part(False, info_other, own_next, own_prev, *sums)
+        sums = own_part(None, info_other, own_next, own_prev, *sums_0, *sums_1)
     cols = ROWS // PARTS
     joined = []
     for i in range(PARTS):
@@ -379,7 +400,7 @@
                 ],
                 compiler_params=params,
                 cost_estimate=cost,
-            )(stretch, query, earlier_far, earlier_prev, *sums)
+            )(stretch, query, earlier_prev, earlier_far, *sums)
         joined.append(lax.all_to_all(part, SHARE, split_axis=0, concat_axis=0, tiled=True))
     with jax.named_scope("join_parts"):
         return pl.pallas_call(

time: 112 us -> 110 us (0.982)
  the two profiles are of different devices: /device:TPU:2 before, /device:TPU:64 now
where the time goes in v4:
time: 110 us; the launch traced here: 109 us
  blocking collectives  62.8 us (57%)
  starting transfers between devices  20.2 us (18%)
  Pallas kernels  14.1 us (13%)
  waiting for transfers between devices  7.17 us (7%)
  local copies, waits for them, and re-layouts  3.51 us (3%)
  other arithmetic  1.19 us (1%)
    all_gather x1, blocking collectives, body(): far = lax.all_gather(own, DEPTH, axis=0, axis_index_groups=FAR)  40.8 us
    all_to_all x1, blocking collectives, body(): lax.all_to_all(part, SHARE, split_axis=0, concat_axis=0, tiled=True)  22 us
    ppermute x4, starting transfers between devices, along(): return lax.ppermute(block, axis, route)  11.9 us
    pallas_call x3, Pallas kernels, own_part(): pl.pallas_call(functools.partial(own_kernel, not state_in, core), out_sha...  10.8 us
    ppermute x4, waiting for transfers between devices, along(): return lax.ppermute(block, axis, route)  4.7 us
    all_to_all x1, starting transfers between devices, body(): own = lax.all_to_all(kv, LINE, split_axis=0, concat_axis=0, tiled=True)  4.46 us
    all_to_all x1, starting transfers between devices, body(): lax.all_to_all(split, SHARE, split_axis=0, concat_axis=0, tiled=True)  3.8 us
    all_to_all x1, waiting for transfers between devices, body(): own = lax.all_to_all(kv, LINE, split_axis=0, concat_axis=0, tiled=True)  2.47 us
  transfers between devices with their start and end apart: 6, of which 2 were waited for; matrix products, arithmetic and copies ran while one was open for 1% of the time, Pallas kernels for 11%

profile of v4, /device:TPU:64, one launch (start us, length us, event | category | flops | bytes accessed | tf_op | source)
XLA Modules:
  0.0 109.2 jit_solution(7317500372087475559)
XLA Ops:
  0.0 0.0 copy-start
  0.0 0.8 fusion.2
  0.8 0.8 fusion.3
  1.6 0.7 pad_maximum_fusion
  2.3 4.5 %all-to-all-start = ((bf16[4,64,256]{2,1,0:T(8,128)(2,1)}), bf16[4,64,256]{2,1,0:T(8,128)(2,1)S(1)}, u32[]{:S(2)}, u32[]{:S(2)}) async-start(bf16[4,64,256]{2,1,0:T(8,128)(2,1)} %pad_maximum_fusion), calls=%async_computation | async-start | bytes 262144 | tf_op jit(solution)/shard_map/all_to_all | solution.py:320
  6.7 0.0 copy-done
  6.8 0.1 reshape.20
  6.9 0.1 constant_dynamic-slice_fusion.2
  6.9 0.1 copy.11
  7.1 0.1 rev.3
  7.2 0.1 copy.12
  7.3 0.1 lt.40
  7.4 0.2 convert_reduce_fusion
  7.6 0.1 select_reduce_fusion
  7.8 0.1 reshape.21
  7.9 0.2 convert_reduce_fusion.1
  8.1 0.1 concatenate.19
  8.2 0.0 copy-start.1
  8.2 1.0 copy-done.1
  9.2 1.0 pack_queries.1
  10.2 2.5 %all-to-all-done = bf16[4,64,256]{2,1,0:T(8,128)(2,1)S(1)} async-done(((bf16[4,64,256]{2,1,0:T(8,128)(2,1)}), bf16[4,64,256]{2,1,0:T(8,128)(2,1)S(1)}, u32[]{:S(2)}, u32[]{:S(2)}) %all-to-all-start) | async-done | bytes 131104 | tf_op jit(solution)/shard_map/all_to_all | solution.py:320
  12.7 3.8 %all-to-all-start.1 = ((bf16[8,64,1024]{2,1,0:T(8,128)(2,1)}), bf16[8,64,1024]{2,1,0:T(8,128)(2,1)S(1)}, u32[]{:S(2)}, u32[]{:S(2)}) async-start(bf16[8,64,1024]{2,1,0:T(8,128)(2,1)} %pack_queries.1), calls=%async_computation.1 | async-start | bytes 2097152 | tf_op jit(solution)/shard_map/all_to_all | solution.py:339
  16.5 40.8 %all-gather = bf16[16,64,256]{2,1,0:T(8,128)(2,1)S(1)} all-gather(bf16[4,64,256]{2,1,0:T(8,128)(2,1)S(1)} %all-to-all-done), channel_id=2, replica_groups={{0,32,64,96},{104,72,40,8},{16,48,80,112},{120,88,56,24},{1,33,65,97},{..., dimensions={0}, use_global_device_ids=true | all-gather | bytes 655360 | tf_op jit(solution)/shard_map/all_gather | solution.py:335
  57.4 1.9 %collective-permute-start = (bf16[4,2,64,256]{3,2,1,0:T(8,128)(2,1)S(1)}, bf16[4,2,64,256]{3,2,1,0:T(8,128)(2,1)S(1)}, u32[]{:S(2)}, u32[]{:S(2)}) collective-permute-start(bf16[4,2,64,256]{3,2,1,0:T(8,128)(2,1)S(1)} %get-tuple-element.41.refs_2_), channel_id=1, source_target_pairs={{0,16},{16,32},{32,48},{48,64},{64,80},{80,96},{96,112},{112,0},{1... | collective-permute-start | bytes 786440 | tf_op jit(solution)/shard_map/ppermute | solution.py:303
  59.3 4.8 %collective-permute-start.3 = (bf16[4,2,64,256]{3,2,1,0:T(8,128)(2,1)S(1)}, bf16[4,2,64,256]{3,2,1,0:T(8,128)(2,1)S(1)}, u32[]{:S(2)}, u32[]{:S(2)}) collective-permute-start(bf16[4,2,64,256]{3,2,1,0:T(8,128)(2,1)S(1)} %get-tuple-element.40.refs_1_), channel_id=1, source_target_pairs={{0,112},{16,0},{32,16},{48,32},{64,48},{80,64},{96,80},{112,96},{1... | collective-permute-start | bytes 786440 | tf_op jit(solution)/shard_map/ppermute | solution.py:303
  64.1 0.0 all-to-all-done.1.refs_0_.q_ref
  64.1 0.6 own_near_core_1.1
  64.7 4.7 %collective-permute-done.refs_2_ = bf16[4,2,64,256]{3,2,1,0:T(8,128)(2,1)S(1)} collective-permute-done((bf16[4,2,64,256]{3,2,1,0:T(8,128)(2,1)S(1)}, bf16[4,2,64,256]{3,2,1,0:T(8,128)(2,1)S(1)}, u32[]{:S(2)}, u32[]{:S(2)}) %collective-permute-start) | collective-permute-done | bytes 262176 | tf_op jit(solution)/shard_map/ppermute | solution.py:303
  69.4 1.3 %collective-permute-start.1 = (bf16[4,2,64,256]{3,2,1,0:T(8,128)(2,1)S(1)}, bf16[4,2,64,256]{3,2,1,0:T(8,128)(2,1)S(1)}, u32[]{:S(2)}, u32[]{:S(2)}) collective-permute-start(bf16[4,2,64,256]{3,2,1,0:T(8,128)(2,1)S(1)} %collective-permute-done.refs_2_), channel_id=1, source_target_pairs={{0,1},{1,2},{2,3},{3,4},{4,5},{5,6},{6,7},{8,9},{9,10},{10,11},{11... | collective-permute-start | bytes 786440 | tf_op jit(solution)/shard_map/ppermute | solution.py:303
  70.7 3.9 %collective-permute-start.2 = (bf16[4,2,64,256]{3,2,1,0:T(8,128)(2,1)S(1)}, bf16[4,2,64,256]{3,2,1,0:T(8,128)(2,1)S(1)}, u32[]{:S(2)}, u32[]{:S(2)}) collective-permute-start(bf16[4,2,64,256]{3,2,1,0:T(8,128)(2,1)S(1)} %get-tuple-element.41.refs_2_), channel_id=1, source_target_pairs={{0,1},{1,2},{2,3},{3,4},{4,5},{5,6},{6,7},{8,9},{9,10},{10,11},{11... | collective-permute-start | bytes 786440 | tf_op jit(solution)/shard_map/ppermute | solution.py:303
  74.6 5.0 %own_near_core_0.1 = (f32[8,1,512]{2,1,0:T(1,128)S(1)}, f32[8,1,512]{2,1,0:T(1,128)S(1)}, f32[8,128,512]{2,1,0:T(8,128)S(1)}) custom-call(s32[49]{0:T(128)S(1)} %get-tuple-element.31.info_ref, bf16[8,64,1024]{2,1,0:T(8,128)(2,1)S(1)} %all-to-all-done.1.refs_0_.q_ref, bf16[4,2,64,256]{3,2,1,0:T(8,128)(2,1)S(1)} %get-tuple-element.40.refs_1_, ...), custom_call_target="tpu_custom_call" | custom-call | flops 2147483648 | bytes 4194304 | tf_op jit(solution)/shard_map/own_near_core_0/pallas_call | solution.py:356
  79.7 0.0 collective-permute-done.3.refs_1_
  79.7 5.2 %own_other.1 = (f32[8,1,512]{2,1,0:T(1,128)S(1)}, f32[8,1,512]{2,1,0:T(1,128)S(1)}, f32[8,128,512]{2,1,0:T(8,128)S(1)}) custom-call(s32[49]{0:T(128)S(1)} %get-tuple-element.38.info_ref, bf16[8,64,1024]{2,1,0:T(8,128)(2,1)S(1)} %all-to-all-done.1.refs_0_.q_ref, bf16[4,2,64,256]{3,2,1,0:T(8,128)(2,1)S(1)} %collective-permute-done.3.refs_1_, ...), custom_call_target="tpu_custom_call" | custom-call | flops 2147483648 | bytes 4194304 | tf_op jit(solution)/shard_map/own_other/pallas_call | solution.py:356
  84.9 0.0 collective-permute-done.1.far_ref
  84.9 0.0 collective-permute-done.2.prev_ref
  84.9 0.9 earlier_part.1
  85.9 22.0 %all_to_all.15.refs_0_ = bf16[8,528,128]{2,1,0:T(8,128)(2,1)S(1)} all-to-all(bf16[8,528,128]{2,1,0:T(8,128)(2,1)S(1)} %earlier_part.1), channel_id=1, replica_groups=mesh['yh'=2,'yl'=2,'za'=4,'zb'=2,'zp'=2,'x'=4,'c'=2] {'yh','yl','zp'}, dimensions={0} | all-to-all | bytes 2162688 | tf_op jit(solution)/shard_map/all_to_all | solution.py:404
  107.8 1.3 %join_parts.1 = bf16[64,4096]{1,0:T(8,128)(2,1)} custom-call(bf16[8,528,128]{2,1,0:T(8,128)(2,1)S(1)} %all_to_all.15.refs_0_), custom_call_target="tpu_custom_call" | custom-call | flops 786432 | bytes 2097152 | tf_op jit(solution)/shard_map/join_parts/pallas_call | solution.py:406
  (11 shorter events, 0.1 us)
Async XLA Ops:
  0.0 6.7 %copy-start = (s32[2,32,8]{1,2,0:T(8,128)S(1)}, s32[2,32,8]{1,2,0:T(8,128)}, u32[]{:S(2)}) copy-start(s32[2,32,8]{1,2,0:T(8,128)} %param.7) | copy-start | bytes 6148
  2.3 10.4 %all-to-all-start = ((bf16[4,64,256]{2,1,0:T(8,128)(2,1)}), bf16[4,64,256]{2,1,0:T(8,128)(2,1)S(1)}, u32[]{:S(2)}, u32[]{:S(2)}) async-start(bf16[4,64,256]{2,1,0:T(8,128)(2,1)} %pad_maximum_fusion), calls=%async_computation | async-start | bytes 262144 | tf_op jit(solution)/shard_map/all_to_all | solution.py:320
  8.2 1.0 copy-start.1
  12.7 51.4 %all-to-all-start.1 = ((bf16[8,64,1024]{2,1,0:T(8,128)(2,1)}), bf16[8,64,1024]{2,1,0:T(8,128)(2,1)S(1)}, u32[]{:S(2)}, u32[]{:S(2)}) async-start(bf16[8,64,1024]{2,1,0:T(8,128)(2,1)} %pack_queries.1), calls=%async_computation.1 | async-start | bytes 2097152 | tf_op jit(solution)/shard_map/all_to_all | solution.py:339
  57.4 12.0 %collective-permute-start = (bf16[4,2,64,256]{3,2,1,0:T(8,128)(2,1)S(1)}, bf16[4,2,64,256]{3,2,1,0:T(8,128)(2,1)S(1)}, u32[]{:S(2)}, u32[]{:S(2)}) collective-permute-start(bf16[4,2,64,256]{3,2,1,0:T(8,128)(2,1)S(1)} %get-tuple-element.41.refs_2_), channel_id=1, source_target_pairs={{0,16},{16,32},{32,48},{48,64},{64,80},{80,96},{96,112},{112,0},{1... | collective-permute-start | bytes 786440 | tf_op jit(solution)/shard_map/ppermute | solution.py:303
  59.3 20.4 %collective-permute-start.3 = (bf16[4,2,64,256]{3,2,1,0:T(8,128)(2,1)S(1)}, bf16[4,2,64,256]{3,2,1,0:T(8,128)(2,1)S(1)}, u32[]{:S(2)}, u32[]{:S(2)}) collective-permute-start(bf16[4,2,64,256]{3,2,1,0:T(8,128)(2,1)S(1)} %get-tuple-element.40.refs_1_), channel_id=1, source_target_pairs={{0,112},{16,0},{32,16},{48,32},{64,48},{80,64},{96,80},{112,96},{1... | collective-permute-start | bytes 786440 | tf_op jit(solution)/shard_map/ppermute | solution.py:303
  69.4 15.5 %collective-permute-start.1 = (bf16[4,2,64,256]{3,2,1,0:T(8,128)(2,1)S(1)}, bf16[4,2,64,256]{3,2,1,0:T(8,128)(2,1)S(1)}, u32[]{:S(2)}, u32[]{:S(2)}) collective-permute-start(bf16[4,2,64,256]{3,2,1,0:T(8,128)(2,1)S(1)} %collective-permute-done.refs_2_), channel_id=1, source_target_pairs={{0,1},{1,2},{2,3},{3,4},{4,5},{5,6},{6,7},{8,9},{9,10},{10,11},{11... | collective-permute-start | bytes 786440 | tf_op jit(solution)/shard_map/ppermute | solution.py:303
  70.7 14.2 %collective-permute-start.2 = (bf16[4,2,64,256]{3,2,1,0:T(8,128)(2,1)S(1)}, bf16[4,2,64,256]{3,2,1,0:T(8,128)(2,1)S(1)}, u32[]{:S(2)}, u32[]{:S(2)}) collective-permute-start(bf16[4,2,64,256]{3,2,1,0:T(8,128)(2,1)S(1)} %get-tuple-element.41.refs_2_), channel_id=1, source_target_pairs={{0,1},{1,2},{2,3},{3,4},{4,5},{5,6},{6,7},{8,9},{9,10},{10,11},{11... | collective-permute-start | bytes 786440 | tf_op jit(solution)/shard_map/ppermute | solution.py:303

commit v5 on v3

--- a/solution.py
+++ b/solution.py
@@ -58,9 +58,24 @@
             out_ref[m * copies + i] = q_ref[:, m * width : (m + 1) * width]
 
 
-def own_kernel(first, info_ref, q_ref, lower_ref, upper_ref, *refs):
-    if not first:
-        state_in, refs = refs[:3], refs[3:]
+def core_of(info_ref):
+    return lax.rem(info_ref[info_ref.shape[0] - 1], 2)
+
+
+def own_kernel(stage, info_ref, *refs):
+    if stage == 1:
+
+        @pl.when(core_of(info_ref) == 0)
+        def _():
+            attend_own(stage, info_ref, *refs)
+
+    else:
+        attend_own(stage, info_ref, *refs)
+
+
+def attend_own(stage, info_ref, q_ref, lower_ref, upper_ref, *refs):
+    states = [refs[3 * i : 3 * i + 3] for i in range(stage)]
+    refs = refs[3 * stage :]
     top_ref, total_ref, sum_ref, k_s, v_s, vt_s, lead_s, score_s, top_s, piece_s, piece_top = refs
     half = lower_ref.shape[0] * 2
     for i in range(2 * half):
@@ -80,13 +95,16 @@
     pairs = blocks // 2
     lower = count // 2
     numbers, queries, seen = 2 * half, 4 * half, 4 * half + blocks
-    if first:
+    if stage == 0:
         top_ref[...] = jnp.full(top_ref.shape, LOW, jnp.float32)
         total_ref[...] = jnp.zeros(total_ref.shape, jnp.float32)
         sum_ref[...] = jnp.zeros(sum_ref.shape, jnp.float32)
-    else:
-        for ref, ref_in in zip((top_ref, total_ref, sum_ref), state_in):
-            ref[...] = ref_in[...]
+    for at, state in enumerate(states):
+
+        @pl.when(core_of(info_ref) == at)
+        def _(state=state):
+            for ref, ref_in in zip((top_ref, total_ref, sum_ref), state):
+                ref[...] = ref_in[...]
 
     def add(b, values_t, scores, top_new):
         old = top_ref[b]
@@ -137,27 +155,42 @@
         at = pl.ds(pl.multiple_of(chunk * CHUNK, CHUNK), CHUNK)
         add(b, vt_s[:, at], piece_s[slot], piece_top[slot])
 
-    begin(pairs, 0)
-    begin(pairs + 1, 1)
-    begin(pairs + 2, 2)
-    end(pairs, 0)
-    begin(pairs + 3, 3)
-    end(pairs + 1, 1)
-    begin_item(0, 0)
-    end(pairs + 2, 2)
-    begin_item(1, 1)
-    end(pairs + 3, 3)
-
-    @pl.loop(0, items // 4)
-    def _(i):
-        begin_item(4 * i + 2, 2)
-        begin_item(4 * i + 3, 3)
-        end_item(4 * i, 0)
-        end_item(4 * i + 1, 1)
-        begin_item(jnp.minimum(4 * i + 4, items - 1), 0)
-        begin_item(jnp.minimum(4 * i + 5, items - 1), 1)
-        end_item(4 * i + 2, 2)
-        end_item(4 * i + 3, 3)
+    if stage != 1:
+        begin(pairs, 0)
+        begin(pairs + 1, 1)
+        begin(pairs + 2, 2)
+        end(pairs, 0)
+        begin(pairs + 3, 3)
+        end(pairs + 1, 1)
+    if stage == 2:
+        begin_item(0, 0)
+    if stage != 1:
+        end(pairs + 2, 2)
+    if stage == 2:
+        begin_item(1, 1)
+    if stage != 1:
+        end(pairs + 3, 3)
+
+    def all_items():
+        if stage != 2:
+            begin_item(0, 0)
+            begin_item(1, 1)
+
+        @pl.loop(0, items // 4)
+        def _(i):
+            begin_item(4 * i + 2, 2)
+            begin_item(4 * i + 3, 3)
+            end_item(4 * i, 0)
+            end_item(4 * i + 1, 1)
+            begin_item(jnp.minimum(4 * i + 4, items - 1), 0)
+            begin_item(jnp.minimum(4 * i + 5, items - 1), 1)
+            end_item(4 * i + 2, 2)
+            end_item(4 * i + 3, 3)
+
+    if stage == 0:
+        pl.when(core_of(info_ref) == 1)(all_items)
+    else:
+        all_items()
 
 
 def earlier_kernel(
@@ -277,7 +310,8 @@
     in_order = jnp.sum(jnp.where(there, keys[:, None, :], 0), axis=2)
     seen = jnp.sum(keys[:, None, :] <= queries[None, :, None], axis=2, dtype=jnp.int32)
     queries = jnp.broadcast_to(queries, seen.shape)
-    table = jnp.concatenate([place, in_order, queries, seen], axis=1)
+    stretches = jnp.broadcast_to(stretch, (2, 1))
+    table = jnp.concatenate([place, in_order, queries, seen, stretches], axis=1)
     return table[0], table[1], stretch.reshape(1)
 
 
@@ -320,8 +354,6 @@
     lower, upper = far[:, :2], far[:, 2:]
     own_next = along(lower, RING, -1, True)
     own_prev = along(upper, RING, 1, True)
-    earlier_far = along(upper, STRETCHES, 1, False)
-    earlier_prev = along(own_prev, STRETCHES, 1, False)
     query = lax.all_to_all(split, SHARE, split_axis=0, concat_axis=0, tiled=True)
     blocks = lines * pairs
 
@@ -338,9 +370,9 @@
     )
     half = count // 2
 
-    def own_part(first, info, lower, upper, *state_in):
+    def own_part(info, lower, upper, *state_in):
         return pl.pallas_call(
-            functools.partial(own_kernel, first),
+            functools.partial(own_kernel, len(state_in) // 3),
             out_shape=state,
             in_specs=[in_smem()] + [in_vmem()] * (3 + len(state_in)),
             out_specs=[in_vmem()] * 3,
@@ -358,10 +390,17 @@
             cost_estimate=cost,
         )(info, query, lower, upper, *state_in)
 
-    with jax.named_scope("own_near"):
-        sums = own_part(True, info_near, lower, upper)
+    with jax.named_scope("own_near_first"):
+        sums_1 = own_part(info_near, lower, upper)
+    onward, *sums_1 = lax.optimization_barrier((upper, *sums_1))
+    own_prev, sums_1[0] = lax.optimization_barrier((own_prev, sums_1[0]))
+    earlier_prev = along(own_prev, STRETCHES, 1, False)
+    earlier_far = along(onward, STRETCHES, 1, False)
+    own_prev, lower, upper = lax.optimization_barrier((own_prev, lower, upper))
+    with jax.named_scope("own_near_second"):
+        sums_0 = own_part(info_near, lower, upper, *sums_1)
     with jax.named_scope("own_other"):
-        sums = own_part(False, info_other, own_next, own_prev, *sums)
+        sums = own_part(info_other, own_next, own_prev, *sums_0, *sums_1)
     cols = ROWS // PARTS
     joined = []
     for i in range(PARTS):
@@ -379,7 +418,7 @@
                 ],
                 compiler_params=params,
                 cost_estimate=cost,
-            )(stretch, query, earlier_far, earlier_prev, *sums)
+            )(stretch, query, earlier_prev, earlier_far, *sums)
         joined.append(lax.all_to_all(part, SHARE, split_axis=0, concat_axis=0, tiled=True))
     with jax.named_scope("join_parts"):
         return pl.pallas_call(

time: 112 us -> 110 us (0.982)
  the two profiles are of different devices: /device:TPU:2 before, /device:TPU:1 now
where the time goes in v5:
time: 110 us; the launch traced here: 109 us
  blocking collectives  54.3 us (49%)
  starting transfers between devices  29.9 us (27%)
  Pallas kernels  19.1 us (17%)
  local copies, waits for them, and re-layouts  3.51 us (3%)
  waiting for transfers between devices  1.33 us (1%)
  other arithmetic  1.19 us (1%)
    all_gather x1, blocking collectives, body(): far = lax.all_gather(own, DEPTH, axis=0, axis_index_groups=FAR)  33.2 us
    all_to_all x1, blocking collectives, body(): lax.all_to_all(part, SHARE, split_axis=0, concat_axis=0, tiled=True)  21.1 us
    ppermute x4, starting transfers between devices, along(): return lax.ppermute(block, axis, route)  20.6 us
    pallas_call x3, Pallas kernels, own_part(): pl.pallas_call(functools.partial(own_kernel, len(state_in) // 3), out_sha...  11 us
    pallas_call x1, Pallas kernels, body(): pl.pallas_call(functools.partial(earlier_kernel, i), out_shape=jax.ShapeD...  5.7 us
    all_to_all x1, starting transfers between devices, body(): own = lax.all_to_all(kv, LINE, split_axis=0, concat_axis=0, tiled=True)  5.01 us
    all_to_all x1, starting transfers between devices, body(): lax.all_to_all(split, SHARE, split_axis=0, concat_axis=0, tiled=True)  4.28 us
  transfers between devices with their start and end apart: 6, of which 1 were waited for; matrix products, arithmetic and copies ran while one was open for 1% of the time, Pallas kernels for 11%

profile of v5, /device:TPU:1, one launch (start us, length us, event | category | flops | bytes accessed | tf_op | source)
XLA Modules:
  0.0 109.5 jit_solution(3950078008425574408)
XLA Ops:
  0.0 0.0 copy-start
  0.0 0.8 fusion.2
  0.8 0.8 fusion.3
  1.6 0.7 pad_maximum_fusion
  2.3 5.0 %all-to-all-start = ((bf16[4,64,256]{2,1,0:T(8,128)(2,1)}), bf16[4,64,256]{2,1,0:T(8,128)(2,1)S(1)}, u32[]{:S(2)}, u32[]{:S(2)}) async-start(bf16[4,64,256]{2,1,0:T(8,128)(2,1)} %pad_maximum_fusion), calls=%async_computation | async-start | bytes 262144 | tf_op jit(solution)/shard_map/all_to_all | solution.py:338
  7.3 0.0 copy-done
  7.3 0.1 reshape.20
  7.4 0.1 constant_dynamic-slice_fusion.2
  7.5 0.1 copy.11
  7.6 0.1 rev.3
  7.8 0.1 copy.12
  7.9 0.1 lt.40
  8.0 0.2 convert_reduce_fusion
  8.2 0.1 select_reduce_fusion
  8.3 0.1 reshape.21
  8.4 0.2 convert_reduce_fusion.1
  8.6 0.1 concatenate.19
  8.7 0.0 copy-start.1
  8.7 1.0 copy-done.1
  9.7 1.0 pack_queries.1
  10.8 1.3 %all-to-all-done = bf16[4,64,256]{2,1,0:T(8,128)(2,1)S(1)} async-done(((bf16[4,64,256]{2,1,0:T(8,128)(2,1)}), bf16[4,64,256]{2,1,0:T(8,128)(2,1)S(1)}, u32[]{:S(2)}, u32[]{:S(2)}) %all-to-all-start) | async-done | bytes 131104 | tf_op jit(solution)/shard_map/all_to_all | solution.py:338
  12.1 4.3 %all-to-all-start.1 = ((bf16[8,64,1024]{2,1,0:T(8,128)(2,1)}), bf16[8,64,1024]{2,1,0:T(8,128)(2,1)S(1)}, u32[]{:S(2)}, u32[]{:S(2)}) async-start(bf16[8,64,1024]{2,1,0:T(8,128)(2,1)} %pack_queries.1), calls=%async_computation.1 | async-start | bytes 2097152 | tf_op jit(solution)/shard_map/all_to_all | solution.py:357
  16.4 33.2 %all-gather = bf16[16,64,256]{2,1,0:T(8,128)(2,1)S(1)} all-gather(bf16[4,64,256]{2,1,0:T(8,128)(2,1)S(1)} %all-to-all-done), channel_id=2, replica_groups={{0,32,64,96},{104,72,40,8},{16,48,80,112},{120,88,56,24},{1,33,65,97},{..., dimensions={0}, use_global_device_ids=true | all-gather | bytes 655360 | tf_op jit(solution)/shard_map/all_gather | solution.py:353
  49.6 5.8 %collective-permute-start = (bf16[4,2,64,256]{3,2,1,0:T(8,128)(2,1)S(1)}, bf16[4,2,64,256]{3,2,1,0:T(8,128)(2,1)S(1)}, u32[]{:S(2)}, u32[]{:S(2)}) collective-permute-start(bf16[4,2,64,256]{3,2,1,0:T(8,128)(2,1)S(1)} %get-tuple-element.41.refs_2_), channel_id=1, source_target_pairs={{0,16},{16,32},{32,48},{48,64},{64,80},{80,96},{96,112},{112,0},{1... | collective-permute-start | bytes 786440 | tf_op jit(solution)/shard_map/ppermute | solution.py:321
  55.4 2.4 %collective-permute-start.3 = (bf16[4,2,64,256]{3,2,1,0:T(8,128)(2,1)S(1)}, bf16[4,2,64,256]{3,2,1,0:T(8,128)(2,1)S(1)}, u32[]{:S(2)}, u32[]{:S(2)}) collective-permute-start(bf16[4,2,64,256]{3,2,1,0:T(8,128)(2,1)S(1)} %get-tuple-element.40.refs_1_), channel_id=1, source_target_pairs={{0,112},{16,0},{32,16},{48,32},{64,48},{80,64},{96,80},{112,96},{1... | collective-permute-start | bytes 786440 | tf_op jit(solution)/shard_map/ppermute | solution.py:321
  57.8 0.0 all-to-all-done.1.refs_0_.q_ref
  57.8 5.2 %own_near_first.1 = (f32[8,1,512]{2,1,0:T(1,128)S(1)}, f32[8,1,512]{2,1,0:T(1,128)S(1)}, f32[8,128,512]{2,1,0:T(8,128)S(1)}) custom-call(s32[49]{0:T(128)S(1)} %get-tuple-element.31.info_ref, bf16[8,64,1024]{2,1,0:T(8,128)(2,1)S(1)} %all-to-all-done.1.refs_0_.q_ref, bf16[4,2,64,256]{3,2,1,0:T(8,128)(2,1)S(1)} %get-tuple-element.40.refs_1_, ...), custom_call_target="tpu_custom_call" | custom-call | flops 2147483648 | bytes 4194304 | tf_op jit(solution)/shard_map/own_near_first/pallas_call | solution.py:374
  63.1 0.0 collective-permute-done.refs_2_
  63.1 10.5 %collective-permute-start.1 = (bf16[4,2,64,256]{3,2,1,0:T(8,128)(2,1)S(1)}, bf16[4,2,64,256]{3,2,1,0:T(8,128)(2,1)S(1)}, u32[]{:S(2)}, u32[]{:S(2)}) collective-permute-start(bf16[4,2,64,256]{3,2,1,0:T(8,128)(2,1)S(1)} %collective-permute-done.refs_2_), channel_id=1, source_target_pairs={{0,1},{1,2},{2,3},{3,4},{4,5},{5,6},{6,7},{8,9},{9,10},{10,11},{11... | collective-permute-start | bytes 786440 | tf_op jit(solution)/shard_map/ppermute | solution.py:321
  73.6 1.9 %collective-permute-start.2 = (bf16[4,2,64,256]{3,2,1,0:T(8,128)(2,1)S(1)}, bf16[4,2,64,256]{3,2,1,0:T(8,128)(2,1)S(1)}, u32[]{:S(2)}, u32[]{:S(2)}) collective-permute-start(bf16[4,2,64,256]{3,2,1,0:T(8,128)(2,1)S(1)} %get-tuple-element.41.refs_2_), channel_id=1, source_target_pairs={{0,1},{1,2},{2,3},{3,4},{4,5},{5,6},{6,7},{8,9},{9,10},{10,11},{11... | collective-permute-start | bytes 786440 | tf_op jit(solution)/shard_map/ppermute | solution.py:321
  75.5 0.6 own_near_second.1
  76.1 0.0 collective-permute-done.3.refs_1_
  76.1 5.2 %own_other.1 = (f32[8,1,512]{2,1,0:T(1,128)S(1)}, f32[8,1,512]{2,1,0:T(1,128)S(1)}, f32[8,128,512]{2,1,0:T(8,128)S(1)}) custom-call(s32[49]{0:T(128)S(1)} %get-tuple-element.38.info_ref, bf16[8,64,1024]{2,1,0:T(8,128)(2,1)S(1)} %all-to-all-done.1.refs_0_.q_ref, bf16[4,2,64,256]{3,2,1,0:T(8,128)(2,1)S(1)} %collective-permute-done.3.refs_1_, ...), custom_call_target="tpu_custom_call" | custom-call | flops 2147483648 | bytes 4194304 | tf_op jit(solution)/shard_map/own_other/pallas_call | solution.py:374
  81.3 0.0 collective-permute-done.1.far_ref
  81.3 0.0 collective-permute-done.2.prev_ref
  81.3 5.7 %earlier_part.1 = bf16[8,528,128]{2,1,0:T(8,128)(2,1)S(1)} custom-call(s32[1]{0:T(128)} %bitcast.10.info_ref, bf16[8,64,1024]{2,1,0:T(8,128)(2,1)S(1)} %all-to-all-done.1.refs_0_.q_ref, bf16[4,2,64,256]{3,2,1,0:T(8,128)(2,1)S(1)} %collective-permute-done.1.far_ref, bf16[4,2,64,256]{3,2,1,0:T(8,128)(2,1)S(1)} %collective-permute-done.2.prev_ref, ...), custom_call_target="tpu_custom_call" | custom-call | flops 2147483648 | bytes 4194304 | tf_op jit(solution)/shard_map/earlier_part/pallas_call | solution.py:408
  87.0 21.1 %all_to_all.15.refs_0_ = bf16[8,528,128]{2,1,0:T(8,128)(2,1)S(1)} all-to-all(bf16[8,528,128]{2,1,0:T(8,128)(2,1)S(1)} %earlier_part.1), channel_id=1, replica_groups=mesh['yh'=2,'yl'=2,'za'=4,'zb'=2,'zp'=2,'x'=4,'c'=2] {'yh','yl','zp'}, dimensions={0} | all-to-all | bytes 2162688 | tf_op jit(solution)/shard_map/all_to_all | solution.py:422
  108.1 1.3 %join_parts.1 = bf16[64,4096]{1,0:T(8,128)(2,1)} custom-call(bf16[8,528,128]{2,1,0:T(8,128)(2,1)S(1)} %all_to_all.15.refs_0_), custom_call_target="tpu_custom_call" | custom-call | flops 786432 | bytes 2097152 | tf_op jit(solution)/shard_map/join_parts/pallas_call | solution.py:424
  (11 shorter events, 0.1 us)
Async XLA Ops:
  0.0 7.3 %copy-start = (s32[2,32,8]{1,2,0:T(8,128)S(1)}, s32[2,32,8]{1,2,0:T(8,128)}, u32[]{:S(2)}) copy-start(s32[2,32,8]{1,2,0:T(8,128)} %param.7) | copy-start | bytes 6148
  2.3 9.8 %all-to-all-start = ((bf16[4,64,256]{2,1,0:T(8,128)(2,1)}), bf16[4,64,256]{2,1,0:T(8,128)(2,1)S(1)}, u32[]{:S(2)}, u32[]{:S(2)}) async-start(bf16[4,64,256]{2,1,0:T(8,128)(2,1)} %pad_maximum_fusion), calls=%async_computation | async-start | bytes 262144 | tf_op jit(solution)/shard_map/all_to_all | solution.py:338
  8.7 1.0 copy-start.1
  12.1 45.7 %all-to-all-start.1 = ((bf16[8,64,1024]{2,1,0:T(8,128)(2,1)}), bf16[8,64,1024]{2,1,0:T(8,128)(2,1)S(1)}, u32[]{:S(2)}, u32[]{:S(2)}) async-start(bf16[8,64,1024]{2,1,0:T(8,128)(2,1)} %pack_queries.1), calls=%async_computation.1 | async-start | bytes 2097152 | tf_op jit(solution)/shard_map/all_to_all | solution.py:357
  49.6 13.4 %collective-permute-start = (bf16[4,2,64,256]{3,2,1,0:T(8,128)(2,1)S(1)}, bf16[4,2,64,256]{3,2,1,0:T(8,128)(2,1)S(1)}, u32[]{:S(2)}, u32[]{:S(2)}) collective-permute-start(bf16[4,2,64,256]{3,2,1,0:T(8,128)(2,1)S(1)} %get-tuple-element.41.refs_2_), channel_id=1, source_target_pairs={{0,16},{16,32},{32,48},{48,64},{64,80},{80,96},{96,112},{112,0},{1... | collective-permute-start | bytes 786440 | tf_op jit(solution)/shard_map/ppermute | solution.py:321
  55.4 20.6 %collective-permute-start.3 = (bf16[4,2,64,256]{3,2,1,0:T(8,128)(2,1)S(1)}, bf16[4,2,64,256]{3,2,1,0:T(8,128)(2,1)S(1)}, u32[]{:S(2)}, u32[]{:S(2)}) collective-permute-start(bf16[4,2,64,256]{3,2,1,0:T(8,128)(2,1)S(1)} %get-tuple-element.40.refs_1_), channel_id=1, source_target_pairs={{0,112},{16,0},{32,16},{48,32},{64,48},{80,64},{96,80},{112,96},{1... | collective-permute-start | bytes 786440 | tf_op jit(solution)/shard_map/ppermute | solution.py:321
  63.1 18.2 %collective-permute-start.1 = (bf16[4,2,64,256]{3,2,1,0:T(8,128)(2,1)S(1)}, bf16[4,2,64,256]{3,2,1,0:T(8,128)(2,1)S(1)}, u32[]{:S(2)}, u32[]{:S(2)}) collective-permute-start(bf16[4,2,64,256]{3,2,1,0:T(8,128)(2,1)S(1)} %collective-permute-done.refs_2_), channel_id=1, source_target_pairs={{0,1},{1,2},{2,3},{3,4},{4,5},{5,6},{6,7},{8,9},{9,10},{10,11},{11... | collective-permute-start | bytes 786440 | tf_op jit(solution)/shard_map/ppermute | solution.py:321
  73.6 7.7 %collective-permute-start.2 = (bf16[4,2,64,256]{3,2,1,0:T(8,128)(2,1)S(1)}, bf16[4,2,64,256]{3,2,1,0:T(8,128)(2,1)S(1)}, u32[]{:S(2)}, u32[]{:S(2)}) collective-permute-start(bf16[4,2,64,256]{3,2,1,0:T(8,128)(2,1)S(1)} %get-tuple-element.41.refs_2_), channel_id=1, source_target_pairs={{0,1},{1,2},{2,3},{3,4},{4,5},{5,6},{6,7},{8,9},{9,10},{10,11},{11... | collective-permute-start | bytes 786440 | tf_op jit(solution)/shard_map/ppermute | solution.py:321
